TPU v7x, 256 devices: a whole 4x4x8 slice. The times are simulated.
256 devices in a mesh: sec: 256 (over y, x, z, core).
Axes of the slice: x: 4, y: 4, z: 8, core: 2. Of those that a mesh axis runs over, the one named last changes fastest.
Arguments:
- front_reflect: float32 [256, 384, 384], P('sec'), may hold values from -0.125 to 0.125
- front_through: float32 [256, 384, 384], P('sec'), may hold values from -1 to 1
- back_reflect: float32 [256, 384, 384], P('sec'), may hold values from -0.125 to 0.125
- back_through: float32 [256, 384, 384], P('sec'), may hold values from -1 to 1
- depth_maps: float32 [256, 4, 384, 384], P('sec'), may hold values from -1 to 1
- incident: float32 [384, 128], replicated, may hold values from -6 to 6
Outputs:
- through_field: float32 [256, 384, 128], P('sec')
- reflected: float32 [256, 384, 128], P('sec')
- depth_fields: float32 [256, 4, 384, 128], P('sec')
All inputs are finite; a program needn't handle non-finite values.
Results may differ from a plain program's by a relative error of at most 0.00013.
Values sent between devices are 32-bit elements; how exact they have to be, the bound alone decides.
A program may use at most 64 MiB of HBM per device.

v0:
```python
import jax
import jax.numpy as jnp
from jax import lax
from jax.sharding import PartitionSpec as P

SEGMENTS = 3


def passed_along(value, axis, by):
    length = lax.axis_size(axis)
    pairs = [(i, i + by) for i in range(length) if 0 <= i + by < length]
    return lax.ppermute(value, axis, pairs)


def product(former, latter):
    return jnp.dot(
        former, latter, precision=lax.Precision.HIGH, preferred_element_type=jnp.float32
    )


def series(bounce, identity):
    partial_value = identity + bounce
    partial_value = identity + product(bounce, partial_value)
    return (partial_value, identity + product(bounce, partial_value))


def combine(upper, lower, complete):
    upper_reflect, upper_through, upper_mirror, upper_return = upper
    lower_reflect, lower_through, lower_mirror, lower_return = lower
    identity = jnp.eye(lower_reflect.shape[0], dtype=jnp.float32)
    partial_value, forward_sum = series(product(upper_mirror, lower_reflect), identity)
    g_through = product(forward_sum, upper_through)
    new_through = product(lower_through, g_through)
    new_reflect = upper_reflect + product(upper_return, product(lower_reflect, g_through))
    if not complete:
        return (new_reflect, new_through)
    reverse_sum = series(product(lower_reflect, upper_mirror), identity)[1]
    h_return = product(reverse_sum, lower_return)
    new_return = product(upper_return, h_return)
    new_mirror = lower_mirror + product(lower_through, product(upper_mirror, h_return))
    return (new_reflect, new_through, new_mirror, new_return)


def restore(arrived, missing, identity):
    return (
        arrived[0],
        arrived[1] + missing * identity,
        arrived[2],
        arrived[3] + missing * identity,
    )


def per_device(front_reflect, front_through, back_reflect, back_through, depth_maps, incident):
    stride = lax.axis_size("sec") // 2**SEGMENTS
    position = lax.axis_index("sec")
    identity = jnp.eye(front_reflect.shape[1], dtype=jnp.float32)
    current = (front_reflect[0], front_through[0], back_reflect[0], back_through[0])
    for level_index in range(SEGMENTS - 1):
        distance = stride * 2**level_index
        arrived = passed_along(current, "sec", distance)
        missing = jnp.where(position >= distance, 0.0, 1.0)
        current = combine(restore(arrived, missing, identity), current, True)
    distance = stride * 2 ** (SEGMENTS - 1)
    missing = jnp.where(position >= distance, 0.0, 1.0)
    arrived = passed_along(current, "sec", distance)
    final_reflect, final_through = combine(restore(arrived, missing, identity), current, False)
    through_field = product(final_through, incident)
    reflected = product(final_reflect, incident)
    entering = passed_along(through_field, "sec", 1)
    first_section = jnp.where(position == 0, 1.0, 0.0)
    entering = entering + first_section * incident
    depth_fields = jnp.einsum(
        "jmn,nc->jmc",
        depth_maps[0],
        entering,
        precision=lax.Precision.HIGH,
        preferred_element_type=jnp.float32,
    )
    return (through_field[None], reflected[None], depth_fields[None])


def solution(mesh):
    in_specs = (
        P("sec", None, None),
        P("sec", None, None),
        P("sec", None, None),
        P("sec", None, None),
        P("sec", None, None, None),
        P(),
    )
    out_specs = (P("sec", None, None), P("sec", None, None), P("sec", None, None, None))
    return jax.shard_map(
        per_device, mesh=mesh, in_specs=in_specs, out_specs=out_specs, check_vma=False
    )
```

profile of v0, /device:TPU:2, one launch (start us, length us, event | category | flops | bytes accessed | tf_op | source)
XLA Modules:
  0.0 176.1 jit_solution(16425946299646389322)
XLA Ops:
  0.7 2.3 %copy.9 = f32[1,384,384]{1,2,0:T(8,128)} copy(f32[1,384,384]{2,1,0:T(8,128)} %param.8) | data formatting | bytes 1179648 | tf_op args[2]
  2.9 4.1 %collective-permute-start = (f32[384,384]{0,1:T(8,128)}, f32[384,384]{0,1:T(8,128)S(1)}, u32[]{:S(2)}, u32[]{:S(2)}) collective-permute-start(f32[384,384]{0,1:T(8,128)} %bitcast.93), channel_id=1, source_target_pairs={{0,32},{1,33},{2,34},{3,35},{4,36},{5,37},{6,38},{7,39},{8,40},{9,... | collective-permute-start | bytes 1769480 | tf_op jit(solution)/shard_map/ppermute | solution.py:12
  7.0 5.1 %collective-permute-start.1 = (f32[384,384]{1,0:T(8,128)}, f32[384,384]{1,0:T(8,128)}, u32[]{:S(2)}, u32[]{:S(2)}) collective-permute-start(f32[384,384]{1,0:T(8,128)} %bitcast.92), channel_id=1, source_target_pairs={{0,32},{1,33},{2,34},{3,35},{4,36},{5,37},{6,38},{7,39},{8,40},{9,... | collective-permute-start | bytes 1769480 | tf_op jit(solution)/shard_map/ppermute | solution.py:12
  12.1 4.1 %collective-permute-start.4 = (f32[384,384]{1,0:T(8,128)}, f32[384,384]{1,0:T(8,128)}, u32[]{:S(2)}, u32[]{:S(2)}) collective-permute-start(f32[384,384]{1,0:T(8,128)} %bitcast.94), channel_id=1, source_target_pairs={{0,32},{1,33},{2,34},{3,35},{4,36},{5,37},{6,38},{7,39},{8,40},{9,... | collective-permute-start | bytes 1769480 | tf_op jit(solution)/shard_map/ppermute | solution.py:12
  16.2 4.3 %collective-permute-start.3 = (f32[384,384]{1,0:T(8,128)}, f32[384,384]{1,0:T(8,128)}, u32[]{:S(2)}, u32[]{:S(2)}) collective-permute-start(f32[384,384]{1,0:T(8,128)} %bitcast.91), channel_id=1, source_target_pairs={{0,32},{1,33},{2,34},{3,35},{4,36},{5,37},{6,38},{7,39},{8,40},{9,... | collective-permute-start | bytes 1769480 | tf_op jit(solution)/shard_map/ppermute | solution.py:12
  20.5 0.5 collective-permute-done
  21.0 1.8 %fusion.43 = f32[384,384]{1,0:T(8,128)S(1)} fusion(f32[384,384]{0,1:T(8,128)S(1)} %collective-permute-done, f32[1,384,384]{2,1,0:T(8,128)} %param.6), kind=kOutput, calls=%fused_computation.67 | convolution fusion | flops 339738624 | bytes 1769472 | tf_op jit(solution)/shard_map/dot_general | solution.py:16
  22.8 0.7 convert_add_fusion.13
  23.6 0.7 fusion.41
  24.3 0.7 convert_add_fusion.10
  25.0 0.7 convert_add_fusion.9
  25.8 0.7 fusion.34
  26.5 0.8 copy-done.2
  27.3 0.8 fusion.53
  28.1 1.5 fusion.5
  29.6 0.7 convert_add_fusion.12
  30.3 7.0 %collective-permute-start.2 = (f32[384,384]{0,1:T(8,128)}, f32[384,384]{0,1:T(8,128)}, u32[]{:S(2)}, u32[]{:S(2)}) collective-permute-start(f32[384,384]{0,1:T(8,128)} %fusion.5), channel_id=1, source_target_pairs={{0,64},{1,65},{2,66},{3,67},{4,68},{5,69},{6,70},{7,71},{8,72},{9,... | collective-permute-start | bytes 1769480 | tf_op jit(solution)/shard_map/ppermute | solution.py:12
  37.3 1.8 %fusion.6 = f32[384,384]{1,0:T(8,128)S(1)} fusion(f32[384,384]{1,0:T(8,128)S(1)} %convert_add_fusion.12, f32[384,384]{1,0:T(8,128)} %collective-permute-done.1, f32[]{:T(128)S(6)} %select_n.13), kind=kOutput, calls=%fused_computation.29 | convolution fusion | flops 340180992 | bytes 1769476 | tf_op jit(solution)/shard_map/dot_general | solution.py:16
  39.1 0.8 copy-done.3
  39.9 1.2 fusion.37
  41.1 1.0 copy.10
  42.1 2.7 %collective-permute-start.5 = (f32[384,384]{1,0:T(8,128)}, f32[384,384]{1,0:T(8,128)S(1)}, u32[]{:S(2)}, u32[]{:S(2)}) collective-permute-start(f32[384,384]{1,0:T(8,128)} %bitcast.95), channel_id=1, source_target_pairs={{0,64},{1,65},{2,66},{3,67},{4,68},{5,69},{6,70},{7,71},{8,72},{9,... | collective-permute-start | bytes 1769480 | tf_op jit(solution)/shard_map/ppermute | solution.py:12
  44.8 1.4 collective-permute-done.4
  46.3 1.9 %fusion.11 = f32[384,384]{1,0:T(8,128)S(1)} fusion(f32[384,384]{1,0:T(8,128)} %copy-done.2, f32[384,384]{1,0:T(8,128)} %collective-permute-done.4, f32[]{:T(128)S(6)} %select_n.13), kind=kOutput, calls=%fused_computation.35 | convolution fusion | flops 340180992 | bytes 1769476 | tf_op jit(solution)/shard_map/dot_general | solution.py:16
  48.2 6.6 %collective-permute-start.8 = (f32[384,384]{1,0:T(8,128)S(1)}, f32[384,384]{1,0:T(8,128)S(1)}, u32[]{:S(2)}, u32[]{:S(2)}) collective-permute-start(f32[384,384]{1,0:T(8,128)S(1)} %fusion.11), channel_id=1, source_target_pairs={{0,64},{1,65},{2,66},{3,67},{4,68},{5,69},{6,70},{7,71},{8,72},{9,... | collective-permute-start | bytes 1769480 | tf_op jit(solution)/shard_map/ppermute | solution.py:12
  54.8 2.2 %fusion.39 = f32[384,384]{1,0:T(8,128)S(1)} fusion(f32[384,384]{1,0:T(8,128)} %copy-done.3, f32[1,384,384]{2,1,0:T(8,128)S(1)} %copy-done.1), kind=kOutput, calls=%fused_computation.63 | convolution fusion | flops 339738624 | bytes 1769472 | tf_op jit(solution)/shard_map/dot_general | solution.py:16
  57.0 0.8 collective-permute-done.3
  57.8 2.0 %convolution_add_fusion.1 = f32[384,384]{1,0:T(8,128)S(1)} fusion(f32[384,384]{1,0:T(8,128)} %collective-permute-done.3, f32[384,384]{1,0:T(8,128)S(1)} %fusion.39, f32[384,384]{1,0:T(8,128)} %collective-permute-done.4, f32[]{:T(128)S(6)} %select_n.13), kind=kOutput, calls=%fused_computation.19 | convolution fusion | flops 340328448 | bytes 2359300 | tf_op jit(solution)/shard_map/dot_general | solution.py:16
  59.7 6.4 %collective-permute-start.7 = (f32[384,384]{1,0:T(8,128)S(1)}, f32[384,384]{1,0:T(8,128)S(1)}, u32[]{:S(2)}, u32[]{:S(2)}) collective-permute-start(f32[384,384]{1,0:T(8,128)S(1)} %convolution_add_fusion.1), channel_id=1, source_target_pairs={{0,64},{1,65},{2,66},{3,67},{4,68},{5,69},{6,70},{7,71},{8,72},{9,... | collective-permute-start | bytes 1769480 | tf_op jit(solution)/shard_map/ppermute | solution.py:12
  66.1 6.2 %collective-permute-done.2 = f32[384,384]{0,1:T(8,128)} collective-permute-done((f32[384,384]{0,1:T(8,128)}, f32[384,384]{0,1:T(8,128)}, u32[]{:S(2)}, u32[]{:S(2)}) %collective-permute-start.2) | collective-permute-done | bytes 589856 | tf_op jit(solution)/shard_map/ppermute | solution.py:12
  72.3 1.8 %fusion.54 = f32[384,384]{1,0:T(8,128)S(1)} fusion(f32[384,384]{0,1:T(8,128)} %collective-permute-done.2, f32[384,384]{1,0:T(8,128)S(1)} %convolution_add_fusion.1), kind=kOutput, calls=%fused_computation.78 | convolution fusion | flops 339738624 | bytes 1769472 | tf_op jit(solution)/shard_map/dot_general | solution.py:16
  74.2 0.7 convert_add_fusion.7
  74.9 1.8 %fusion.56 = f32[384,384]{1,0:T(8,128)S(1)} fusion(f32[384,384]{1,0:T(8,128)S(1)} %convolution_add_fusion.1, f32[384,384]{0,1:T(8,128)} %collective-permute-done.2), kind=kOutput, calls=%fused_computation.80 | convolution fusion | flops 339738624 | bytes 1769472 | tf_op jit(solution)/shard_map/dot_general | solution.py:16
  76.7 0.7 convert_add_fusion.4
  77.4 0.7 convert_add_fusion.3
  78.1 0.7 fusion.57
  78.9 1.8 %fusion.58 = f32[384,384]{1,0:T(8,128)S(1)} fusion(f32[384,384]{0,1:T(8,128)} %collective-permute-done.2, f32[384,384]{1,0:T(8,128)S(1)} %fusion.57), kind=kOutput, calls=%fused_computation.82 | convolution fusion | flops 339738624 | bytes 1769472 | tf_op jit(solution)/shard_map/dot_general | solution.py:16
  80.7 1.8 %convolution_add_fusion = f32[384,384]{0,1:T(8,128)S(1)} fusion(f32[384,384]{0,1:T(8,128)} %fusion.5, f32[384,384]{1,0:T(8,128)S(1)} %fusion.37, f32[384,384]{1,0:T(8,128)S(1)} %fusion.58), kind=kOutput, calls=%fused_computation.18 | convolution fusion | flops 339886080 | bytes 2359296 | tf_op jit(solution)/shard_map/dot_general | solution.py:16
  82.5 0.7 convert_add_fusion.6
  83.2 6.0 %collective-permute-start.6 = (f32[384,384]{0,1:T(8,128)S(1)}, f32[384,384]{0,1:T(8,128)S(1)}, u32[]{:S(2)}, u32[]{:S(2)}) collective-permute-start(f32[384,384]{0,1:T(8,128)S(1)} %convolution_add_fusion), channel_id=1, source_target_pairs={{0,128},{1,129},{2,130},{3,131},{4,132},{5,133},{6,134},{7,135},{8... | collective-permute-start | bytes 1769480 | tf_op jit(solution)/shard_map/ppermute | solution.py:12
  89.3 0.7 fusion.7
  90.0 0.8 fusion.55
  90.8 1.6 collective-permute-start.9
  92.4 5.1 %collective-permute-done.8 = f32[384,384]{1,0:T(8,128)S(1)} collective-permute-done((f32[384,384]{1,0:T(8,128)S(1)}, f32[384,384]{1,0:T(8,128)S(1)}, u32[]{:S(2)}, u32[]{:S(2)}) %collective-permute-start.8) | collective-permute-done | bytes 589856 | tf_op jit(solution)/shard_map/ppermute | solution.py:12
  97.5 0.7 fusion.12
  98.2 6.3 %collective-permute-start.11 = (f32[384,384]{1,0:T(8,128)S(1)}, f32[384,384]{1,0:T(8,128)S(1)}, u32[]{:S(2)}, u32[]{:S(2)}) collective-permute-start(f32[384,384]{1,0:T(8,128)S(1)} %fusion.12), channel_id=1, source_target_pairs={{0,128},{1,129},{2,130},{3,131},{4,132},{5,133},{6,134},{7,135},{8... | collective-permute-start | bytes 1769480 | tf_op jit(solution)/shard_map/ppermute | solution.py:12
  104.5 0.7 fusion.59
  105.2 0.7 fusion.13
  105.9 4.2 %collective-permute-done.7 = f32[384,384]{1,0:T(8,128)S(1)} collective-permute-done((f32[384,384]{1,0:T(8,128)S(1)}, f32[384,384]{1,0:T(8,128)S(1)}, u32[]{:S(2)}, u32[]{:S(2)}) %collective-permute-start.7) | collective-permute-done | bytes 589856 | tf_op jit(solution)/shard_map/ppermute | solution.py:12
  110.2 0.1 add.100
  110.2 50.2 %collective-permute-start.10 = (f32[384,384]{1,0:T(8,128)S(1)}, f32[384,384]{1,0:T(8,128)S(1)}, u32[]{:S(2)}, u32[]{:S(2)}) collective-permute-start(f32[384,384]{1,0:T(8,128)S(1)} %add.100), channel_id=1, source_target_pairs={{0,128},{1,129},{2,130},{3,131},{4,132},{5,133},{6,134},{7,135},{8... | collective-permute-start | bytes 1769480 | tf_op jit(solution)/shard_map/ppermute | solution.py:12
  160.4 0.8 fusion.60
  161.2 0.7 convert_add_fusion.1
  161.9 0.7 convert_add_fusion
  162.7 0.7 fusion.8
  163.4 0.7 fusion.61
  164.1 0.4 fusion.62
  164.5 1.9 %collective-permute-start.12 = (f32[384,128]{1,0:T(8,128)S(1)}, f32[384,128]{1,0:T(8,128)S(1)}, u32[]{:S(2)}, u32[]{:S(2)}) collective-permute-start(f32[384,128]{1,0:T(8,128)S(1)} %fusion.62), channel_id=1, source_target_pairs={{0,1},{1,2},{2,3},{3,4},{4,5},{5,6},{6,7},{7,8},{8,9},{9,10},{10,1... | collective-permute-start | bytes 589832 | tf_op jit(solution)/shard_map/ppermute | solution.py:12
  166.4 0.7 fusion.63
  167.2 0.7 fusion.9
  167.9 1.1 convolution_bitcast_fusion.1
  169.0 4.7 %collective-permute-done.12 = f32[384,128]{1,0:T(8,128)S(1)} collective-permute-done((f32[384,128]{1,0:T(8,128)S(1)}, f32[384,128]{1,0:T(8,128)S(1)}, u32[]{:S(2)}, u32[]{:S(2)}) %collective-permute-start.12) | collective-permute-done | bytes 196640 | tf_op jit(solution)/shard_map/ppermute | solution.py:12
  173.6 1.4 fusion.2
  175.0 1.2 copy.12
  (22 shorter events, 0.1 us)
Async XLA Ops:
  0.6 173.0 %copy-start = (f32[1,4,384,384]{3,2,1,0:T(8,128)S(1)}, f32[1,4,384,384]{3,2,1,0:T(8,128)}, u32[]{:S(2)}) copy-start(f32[1,4,384,384]{3,2,1,0:T(8,128)} %param.10) | copy-start | bytes 7077892
  0.6 22.9 %copy-start.1 = (f32[1,384,384]{2,1,0:T(8,128)S(1)}, f32[1,384,384]{2,1,0:T(8,128)}, u32[]{:S(2)}) copy-start(f32[1,384,384]{2,1,0:T(8,128)} %param.6) | copy-start | bytes 1769476
  2.9 18.1 %collective-permute-start = (f32[384,384]{0,1:T(8,128)}, f32[384,384]{0,1:T(8,128)S(1)}, u32[]{:S(2)}, u32[]{:S(2)}) collective-permute-start(f32[384,384]{0,1:T(8,128)} %bitcast.93), channel_id=1, source_target_pairs={{0,32},{1,33},{2,34},{3,35},{4,36},{5,37},{6,38},{7,39},{8,40},{9,... | collective-permute-start | bytes 1769480 | tf_op jit(solution)/shard_map/ppermute | solution.py:12
  7.0 30.3 %collective-permute-start.1 = (f32[384,384]{1,0:T(8,128)}, f32[384,384]{1,0:T(8,128)}, u32[]{:S(2)}, u32[]{:S(2)}) collective-permute-start(f32[384,384]{1,0:T(8,128)} %bitcast.92), channel_id=1, source_target_pairs={{0,32},{1,33},{2,34},{3,35},{4,36},{5,37},{6,38},{7,39},{8,40},{9,... | collective-permute-start | bytes 1769480 | tf_op jit(solution)/shard_map/ppermute | solution.py:12
  12.1 34.2 %collective-permute-start.4 = (f32[384,384]{1,0:T(8,128)}, f32[384,384]{1,0:T(8,128)}, u32[]{:S(2)}, u32[]{:S(2)}) collective-permute-start(f32[384,384]{1,0:T(8,128)} %bitcast.94), channel_id=1, source_target_pairs={{0,32},{1,33},{2,34},{3,35},{4,36},{5,37},{6,38},{7,39},{8,40},{9,... | collective-permute-start | bytes 1769480 | tf_op jit(solution)/shard_map/ppermute | solution.py:12
  16.2 41.6 %collective-permute-start.3 = (f32[384,384]{1,0:T(8,128)}, f32[384,384]{1,0:T(8,128)}, u32[]{:S(2)}, u32[]{:S(2)}) collective-permute-start(f32[384,384]{1,0:T(8,128)} %bitcast.91), channel_id=1, source_target_pairs={{0,32},{1,33},{2,34},{3,35},{4,36},{5,37},{6,38},{7,39},{8,40},{9,... | collective-permute-start | bytes 1769480 | tf_op jit(solution)/shard_map/ppermute | solution.py:12
  23.5 2.2 %copy-start.7 = (f32[1,384,384]{2,1,0:T(8,128)S(1)}, f32[1,384,384]{2,1,0:T(8,128)}, u32[]{:S(2)}) copy-start(f32[1,384,384]{2,1,0:T(8,128)} %param.9) | copy-start | bytes 1769476
  25.0 3.1 %copy-start.4 = (f32[1,384,384]{2,1,0:T(8,128)S(1)}, f32[1,384,384]{2,1,0:T(8,128)}, u32[]{:S(2)}) copy-start(f32[1,384,384]{2,1,0:T(8,128)} %param.7) | copy-start | bytes 1769476
  25.0 3.1 %copy-start.5 = (f32[1,384,384]{1,2,0:T(8,128)S(1)}, f32[1,384,384]{1,2,0:T(8,128)}, u32[]{:S(2)}) copy-start(f32[1,384,384]{1,2,0:T(8,128)} %copy.9) | copy-start | bytes 1769476
  26.5 0.8 copy-start.2
  30.3 42.0 %collective-permute-start.2 = (f32[384,384]{0,1:T(8,128)}, f32[384,384]{0,1:T(8,128)}, u32[]{:S(2)}, u32[]{:S(2)}) collective-permute-start(f32[384,384]{0,1:T(8,128)} %fusion.5), channel_id=1, source_target_pairs={{0,64},{1,65},{2,66},{3,67},{4,68},{5,69},{6,70},{7,71},{8,72},{9,... | collective-permute-start | bytes 1769480 | tf_op jit(solution)/shard_map/ppermute | solution.py:12
  39.1 0.8 copy-start.3
  42.1 47.1 %collective-permute-start.5 = (f32[384,384]{1,0:T(8,128)}, f32[384,384]{1,0:T(8,128)S(1)}, u32[]{:S(2)}, u32[]{:S(2)}) collective-permute-start(f32[384,384]{1,0:T(8,128)} %bitcast.95), channel_id=1, source_target_pairs={{0,64},{1,65},{2,66},{3,67},{4,68},{5,69},{6,70},{7,71},{8,72},{9,... | collective-permute-start | bytes 1769480 | tf_op jit(solution)/shard_map/ppermute | solution.py:12
  48.2 49.3 %collective-permute-start.8 = (f32[384,384]{1,0:T(8,128)S(1)}, f32[384,384]{1,0:T(8,128)S(1)}, u32[]{:S(2)}, u32[]{:S(2)}) collective-permute-start(f32[384,384]{1,0:T(8,128)S(1)} %fusion.11), channel_id=1, source_target_pairs={{0,64},{1,65},{2,66},{3,67},{4,68},{5,69},{6,70},{7,71},{8,72},{9,... | collective-permute-start | bytes 1769480 | tf_op jit(solution)/shard_map/ppermute | solution.py:12
  59.7 50.4 %collective-permute-start.7 = (f32[384,384]{1,0:T(8,128)S(1)}, f32[384,384]{1,0:T(8,128)S(1)}, u32[]{:S(2)}, u32[]{:S(2)}) collective-permute-start(f32[384,384]{1,0:T(8,128)S(1)} %convolution_add_fusion.1), channel_id=1, source_target_pairs={{0,64},{1,65},{2,66},{3,67},{4,68},{5,69},{6,70},{7,71},{8,72},{9,... | collective-permute-start | bytes 1769480 | tf_op jit(solution)/shard_map/ppermute | solution.py:12
  83.2 77.2 %collective-permute-start.6 = (f32[384,384]{0,1:T(8,128)S(1)}, f32[384,384]{0,1:T(8,128)S(1)}, u32[]{:S(2)}, u32[]{:S(2)}) collective-permute-start(f32[384,384]{0,1:T(8,128)S(1)} %convolution_add_fusion), channel_id=1, source_target_pairs={{0,128},{1,129},{2,130},{3,131},{4,132},{5,133},{6,134},{7,135},{8... | collective-permute-start | bytes 1769480 | tf_op jit(solution)/shard_map/ppermute | solution.py:12
  90.8 71.9 %collective-permute-start.9 = (f32[384,384]{1,0:T(8,128)S(1)}, f32[384,384]{1,0:T(8,128)S(1)}, u32[]{:S(2)}, u32[]{:S(2)}) collective-permute-start(f32[384,384]{1,0:T(8,128)S(1)} %fusion.55), channel_id=1, source_target_pairs={{0,128},{1,129},{2,130},{3,131},{4,132},{5,133},{6,134},{7,135},{8... | collective-permute-start | bytes 1769480 | tf_op jit(solution)/shard_map/ppermute | solution.py:12
  98.2 68.9 %collective-permute-start.11 = (f32[384,384]{1,0:T(8,128)S(1)}, f32[384,384]{1,0:T(8,128)S(1)}, u32[]{:S(2)}, u32[]{:S(2)}) collective-permute-start(f32[384,384]{1,0:T(8,128)S(1)} %fusion.12), channel_id=1, source_target_pairs={{0,128},{1,129},{2,130},{3,131},{4,132},{5,133},{6,134},{7,135},{8... | collective-permute-start | bytes 1769480 | tf_op jit(solution)/shard_map/ppermute | solution.py:12
  110.2 57.7 %collective-permute-start.10 = (f32[384,384]{1,0:T(8,128)S(1)}, f32[384,384]{1,0:T(8,128)S(1)}, u32[]{:S(2)}, u32[]{:S(2)}) collective-permute-start(f32[384,384]{1,0:T(8,128)S(1)} %add.100), channel_id=1, source_target_pairs={{0,128},{1,129},{2,130},{3,131},{4,132},{5,133},{6,134},{7,135},{8... | collective-permute-start | bytes 1769480 | tf_op jit(solution)/shard_map/ppermute | solution.py:12
  161.9 2.2 %copy-start.6 = (f32[384,128]{1,0:T(8,128)S(1)}, f32[384,128]{1,0:T(8,128)}, u32[]{:S(2)}) copy-start(f32[384,128]{1,0:T(8,128)} %param.11) | copy-start | bytes 589828
  164.5 4.5 %copy-start.8 = (f32[384,128]{1,0:T(8,128)}, f32[384,128]{1,0:T(8,128)S(1)}, u32[]{:S(2)}) copy-start(f32[384,128]{1,0:T(8,128)S(1)} %fusion.62) | copy-start | bytes 589828
  164.5 9.1 %collective-permute-start.12 = (f32[384,128]{1,0:T(8,128)S(1)}, f32[384,128]{1,0:T(8,128)S(1)}, u32[]{:S(2)}, u32[]{:S(2)}) collective-permute-start(f32[384,128]{1,0:T(8,128)S(1)} %fusion.62), channel_id=1, source_target_pairs={{0,1},{1,2},{2,3},{3,4},{4,5},{5,6},{6,7},{7,8},{8,9},{9,10},{10,1... | collective-permute-start | bytes 589832 | tf_op jit(solution)/shard_map/ppermute | solution.py:12
where the time goes:
time: 177 us; the launch traced here: 176 us
  starting transfers between devices  106 us (60%)
  matrix products  39.6 us (22%)
  waiting for transfers between devices  23 us (13%)
  local copies, waits for them, and re-layouts  6.15 us (3%)
    ppermute x13, starting transfers between devices, passed_along(): return lax.ppermute(value, axis, pairs)  106 us
    dot_general x37, matrix products, product(): jnp.dot(former, latter, precision=lax.Precision.HIGH, preferred_element_t...  38.3 us
    ppermute x13, waiting for transfers between devices, passed_along(): return lax.ppermute(value, axis, pairs)  23 us
    unnamed x20, local copies, waits for them, and re-layouts  5.11 us
  transfers between devices with their start and end apart: 13, of which 7 were waited for; matrix products, arithmetic and copies ran while one was open for 22% of the time, Pallas kernels for 0%

commit v1 on v0

v1 whole, which is shorter than its diff:
```python
import functools

import jax
import jax.numpy as jnp
from jax import lax
from jax.experimental import pallas as pl
from jax.experimental.pallas import tpu as pltpu
from jax.sharding import PartitionSpec as P


F32, BF16 = jnp.float32, jnp.bfloat16
MESH = pl.DeviceIdType.MESH
M, INC, DEPTHS = 384, 128, 4

FQ, FR, FT, FU, LQ, LR, LT, LU = range(8)
CQ, CR, CT, CU = range(8, 12)
DQ, DR, DT, DU, R6, T6 = range(12, 18)
HQ, HU, RIN, ROUT, POUT, R23, Q01, U01, T3, P3, TX, TM, TRP = range(18, 31)
BLOCKS = 31
HT, HR, T01, R01, G2, P1, RB, RC, TA, TB, PL, GL, TL, RL, ENT = range(15)
VECS = 15


def halves(x):
    high = x.astype(BF16)
    return high, (x - high.astype(F32)).astype(BF16)


def left(x):
    high, low = halves(x)
    return jnp.concatenate([high, low, high], axis=1)


def right(x):
    high, low = halves(x)
    return jnp.concatenate([high, high, low], axis=0)


def mm(a, b):
    return jnp.dot(left(a), right(b), preferred_element_type=F32)


def spread(mirror, reflect):
    bounce = mm(mirror, reflect)
    return bounce, bounce + mm(bounce, bounce)


def summed(bounce, both, value):
    partial_value = value + mm(both, value)
    return partial_value, value + mm(bounce, partial_value)


def forward(former, latter_reflect):
    mirror, reflect, through, back = former
    bounce, both = spread(mirror, latter_reflect)
    g_through = summed(bounce, both, through)[1]
    return reflect + mm(back, mm(latter_reflect, g_through)), g_through


def applied(mirror, back, field, reflected, latter_reflect):
    bounce = mm(mirror, latter_reflect)
    value = field
    for _ in range(3):
        value = field + mm(bounce, value)
    return value, reflected + mm(back, mm(latter_reflect, value))


def joined(mirror, back, field, reflected, latter):
    own_mirror, own_reflect, own_through, own_back = latter
    cut = field.shape[1]
    bounce, both = spread(mirror, own_reflect)
    value = jnp.concatenate([field, mm(mirror, own_back)], axis=1)
    partial_value, full_value = summed(bounce, both, value)
    through = mm(own_through, full_value)
    turned = mm(own_reflect, jnp.concatenate([full_value[:, :cut], partial_value[:, cut:]], axis=1))
    returned = mm(back, jnp.concatenate([turned[:, :cut], own_back + turned[:, cut:]], axis=1))
    return (
        through[:, :cut],
        reflected + returned[:, :cut],
        own_mirror + through[:, cut:],
        returned[:, cut:],
    )


def index_of(x, y, z, c):
    return ((y * 4 + x) * 8 + z) * 2 + c


def middle_x(x, c):
    return lax.rem(x + jnp.where(x // 2 == c, 1, 3), 4)


def producer(k_half, y, middle, z):
    at = jnp.where(y == 0, 0, jnp.where(y == 1, k_half, jnp.where(y == 2, 2, 2 + k_half)))
    return index_of(middle, at, z, 1 - k_half)


def kernel(
    reflect_ref, through_ref, mirror_ref, back_ref, maps_ref, incident_ref,
    through_out, reflected_out, depth_out,
    W, V, maps, maps_left, depth, send, recv, local,
):
    me = lax.axis_index("sec")
    c, z, x, y = me % 2, (me // 2) % 8, (me // 16) % 4, me // 64
    x_half = x // 2
    middle = middle_x(x, c)
    base = 1 - x % 2
    group_c = jnp.where(x % 2 == 1, x_half, 1 - x_half)
    residue = base * 16 + z * 2 + group_c
    chain_half = 1 - c

    def col(at_y, at_c):
        return index_of(x, at_y, z, at_c)

    def home(at_y, half):
        return index_of(base + 2 * half, at_y, z, group_c)

    is_a = c == 0
    is_mid = is_a | (y == 0) | (y == 2)
    is_hub = (is_a & (y == 1)) | ((c == 1) & (y == 0))
    is_two = y == 2
    is_a0, is_a2, is_a3 = is_a & (y == 0), is_a & (y == 2), is_a & (y == 3)
    is_b0, is_b2 = (c == 1) & (y == 0), (c == 1) & (y == 2)
    is_last = is_a3 | is_b2
    is_first_home = (x_half == 0) & (y == 0)

    barrier = pltpu.get_barrier_semaphore()

    def greet(condition, device):
        @pl.when(condition)
        def _():
            pl.semaphore_signal(barrier, inc=1, device_id=(device,), device_id_type=MESH)

    def count(condition, n=1):
        return jnp.where(condition, n, 0)

    greet(is_a, home(y, 0))
    greet(is_a, home(y, 1))
    expected = 1
    greet(is_b0 | is_b2, col(y // 2 + 1, 0))
    expected += count(is_a & ((y == 1) | (y == 2)))
    greet(is_b0 | is_b2, col(y // 2, 0))
    expected += count(is_a & (y < 2))
    greet(is_b0, home(0, 0))
    expected += count(is_first_home)
    greet(is_b2, col(3, 0))
    expected += count(is_a3)
    greet(is_a & (y == 1), col(0, 0))
    expected += count(is_a0)
    greet(is_a & ((y == 1) | (y == 2)), col(y + 1, 0))
    greet(is_b0, col(2, 1))
    expected += count((is_a & (y >= 2)) | is_b2)
    greet(is_two, col(1 - c, c))
    expected += count(is_hub)
    greet(is_a3, col(1, 0))
    expected += count(is_a & (y == 1))
    greet(is_a3, col(2, 0))
    expected += count(is_a2)
    greet((y == 0) & (x_half == 1), index_of(middle, 0, z, 0))
    expected += count(is_a0)
    greet(y >= 1, index_of(middle, x_half, z, 1 - x_half))
    expected += count(is_hub, 3)
    greet(y >= 2, producer(x_half, y, middle, z))
    expected += count(is_two) + count(is_last)
    before = jnp.maximum(me - 1, 0)
    bc, bz, bx, by = before % 2, (before // 2) % 8, (before // 16) % 4, before // 64
    first_before = (by == 0) & (bx // 2 == 0)
    greet(
        me >= 1,
        jnp.where(first_before, before, producer(bx // 2, by, middle_x(bx, bc), bz)),
    )
    goes_on = ~(is_a3 & (residue == 31))
    expected += count(is_first_home) + count(is_a0) + count(is_hub) + count(is_two)
    expected += count(is_last & goes_on)

    maps_copy = pltpu.make_async_copy(maps_ref.at[0], maps, local.at[0])
    maps_copy.start()

    @pl.when(is_first_home)
    def _():
        pltpu.make_async_copy(through_ref.at[0], W.at[T3], local.at[1]).start()
        pltpu.make_async_copy(reflect_ref.at[0], W.at[P3], local.at[2]).start()

    pl.semaphore_wait(barrier, expected)

    other = lax.rem(me + 1, lax.axis_size("sec"))

    def message(source, target, s, r, device):
        return pltpu.make_async_remote_copy(
            src_ref=source, dst_ref=target, send_sem=send.at[s], recv_sem=recv.at[r],
            device_id=(device,), device_id_type=MESH,
        )

    finals = []

    def post(condition, source, target, s, r, device):
        @pl.when(condition)
        def _():
            message(source, target, s, r, device).start()

        finals.append((condition, source, s))

    def got(target, r):
        message(target, target, 0, r, other).wait_recv()

    def sent(source, s):
        message(source, source, s, 0, other).wait_send()

    sections = (mirror_ref, reflect_ref, through_ref, back_ref)
    middle_a = index_of(middle, y, z, 0)

    def first_send(part):
        message(
            sections[part].at[0], W.at[4 * x_half + part], part, 4 * x_half + part, middle_a
        ).start()

    def pass_on(part):
        @pl.when(is_a)
        def _():
            got(W.at[FQ + part], FQ + part)
            got(W.at[LQ + part], LQ + part)

        post(is_a & ((y == 1) | (y == 2)), W.at[FQ + part], W.at[LQ + part], 4 + part, LQ + part,
             col(2 * (y - 1), 1))
        post(is_a & (y < 2), W.at[LQ + part], W.at[FQ + part], 8 + part, FQ + part, col(2 * y, 1))
        post(is_a2, W.at[LQ + part], W.at[DQ + part], 8 + part, 8 + part, col(2, 1))
        if part in (0, 3):
            at = 0 if part == 0 else 1
            post(is_a0, W.at[FQ + part], W.at[HQ + at], 4 + part, 14 + at, col(0, 1))
        else:
            post(is_a3, W.at[FQ + part], W.at[R6 + part - 1], 4 + part, 12 + part - 1, col(2, 1))

    first_send(0)
    first_send(1)

    @pl.when(is_first_home)
    def _():
        pltpu.make_async_copy(through_ref.at[0], W.at[T3], local.at[1]).wait()
        pltpu.make_async_copy(reflect_ref.at[0], W.at[P3], local.at[2]).wait()
        V[TL] = mm(W[T3], incident_ref[...])
        V[RL] = mm(W[P3], incident_ref[...])

    post(is_first_home, V.at[TL], V.at[HT], 28, 16, index_of(middle, 0, z, 1))
    post(is_first_home, V.at[RL], V.at[HR], 29, 17, index_of(middle, 0, z, 1))
    post(is_first_home, V.at[TL], V.at[ENT], 30, 25, other)

    maps_copy.wait()
    for j in range(DEPTHS):
        maps_left[j * M : (j + 1) * M, :] = left(maps[j])

    pass_on(0)
    sent(sections[0].at[0], 0)
    first_send(2)
    pass_on(1)
    sent(sections[1].at[0], 1)
    first_send(3)

    @pl.when(is_mid)
    def _():
        @pl.when(c == 1)
        def _():
            for part in (0, 1):
                got(W.at[FQ + part], FQ + part)
                got(W.at[LQ + part], LQ + part)

        bounce, both = spread(W[FQ], W[LR])
        W[TX] = bounce
        W[TM] = both

    pass_on(2)

    @pl.when(is_mid)
    def _():
        @pl.when(c == 1)
        def _():
            got(W.at[FT], FT)
            got(W.at[LT], LT)

        g_through = summed(W[TX], W[TM], W[FT])[1]
        W[CT] = mm(W[LT], g_through)
        W[TRP] = mm(W[LR], g_through)

    pass_on(3)

    @pl.when(is_b2)
    def _():
        for part in range(4):
            got(W.at[DQ + part], 8 + part)
        got(W.at[R6], 12)
        got(W.at[T6], 13)
        W[RIN], W[P3] = forward((W[DQ], W[DR], W[DT], W[DU]), W[R6])

    @pl.when(is_mid)
    def _():
        @pl.when(c == 1)
        def _():
            got(W.at[FU], FU)
            got(W.at[LU], LU)

        W[CR] = W[FR] + mm(W[FU], W[TRP])

    post((is_a & (y >= 2)) | is_b2, W.at[CR], W.at[RIN], 16, 18,
         jnp.where(is_a, col(y - 1, 0), col(0, 1)))

    @pl.when(is_mid)
    def _():
        bounce = W[TX]
        mirrored = mm(W[FQ], W[LU])
        partial_value, full_value = summed(bounce, W[TM], mirrored)
        W[CQ] = W[LQ] + mm(W[LT], full_value)
        W[CU] = mm(W[FU], W[LU] + mm(W[LR], partial_value))

    @pl.when(is_a0)
    def _():
        V[T01] = mm(W[CT], incident_ref[...])
        V[R01] = mm(W[CR], incident_ref[...])

    post(is_a0, V.at[T01], V.at[HT], 14, 16, col(1, 0))
    post(is_a0, W.at[CQ], W.at[HQ], 12, 14, col(1, 0))
    post(is_a0, V.at[R01], V.at[HR], 15, 17, col(1, 0))
    post(is_a0, W.at[CU], W.at[HU], 13, 15, col(1, 0))
    post(is_a0, V.at[T01], V.at[TL], 21, 23, home(0, 1))
    post(is_a0, V.at[R01], V.at[RL], 23, 24, home(0, 1))
    post(is_a0, V.at[T01], V.at[ENT], 22, 25, 32 + residue + 1)

    def turn(step, carry):
        @pl.when((is_hub | is_two) & (step == 2 * c))
        def _():
            @pl.when(~is_b2)
            def _():
                got(W.at[RIN], 18)

            W[ROUT], W[POUT] = forward((W[CQ], W[CR], W[CT], W[CU]), W[RIN])

            @pl.when(is_two)
            def _():
                message(W.at[ROUT], W.at[R23], 17, 19, col(1 - c, c)).start()

            @pl.when(is_a2)
            def _():
                message(W.at[POUT], W.at[POUT], 18, 20, col(3, 0)).start()

        @pl.when(is_hub & (step == 1))
        def _():
            got(V.at[HT], 16)
            got(W.at[HQ], 14)
            got(V.at[HR], 17)
            got(W.at[HU], 15)
            V[T01], V[R01], W[Q01], W[U01] = joined(
                W[HQ], W[HU], V[HT], V[HR], (W[CQ], W[CR], W[CT], W[CU])
            )
            message(V.at[T01], V.at[TL], 21, 23, home(1, chain_half)).start()
            message(V.at[R01], V.at[RL], 23, 24, home(1, chain_half)).start()
            message(V.at[T01], V.at[ENT], 22, 25, 32 * (2 + chain_half) + residue + 1).start()

        return carry

    lax.fori_loop(0, 3, turn, 0)
    finals.append((is_two, W.at[ROUT], 17))
    finals.append((is_a2, W.at[POUT], 18))
    finals.append((is_hub, V.at[T01], 21))
    finals.append((is_hub, V.at[R01], 23))
    finals.append((is_hub, V.at[T01], 22))

    @pl.when(is_b2)
    def _():
        W[T3] = mm(W[T6], W[P3])

    @pl.when(is_hub)
    def _():
        got(W.at[R23], 19)
        V[G2], V[RC] = applied(W[Q01], W[U01], V[T01], V[R01], W[R23])
        value, V[RB] = applied(W[HQ], W[HU], V[HT], V[HR], W[ROUT])
        V[P1] = mm(W[POUT], value)

    post(is_hub, V.at[G2], V.at[GL], 20, 22, jnp.where(is_a, col(3, 0), col(2, 1)))
    post(is_hub, V.at[P1], V.at[PL], 19, 21, col(2, c))
    post(is_hub, V.at[RC], V.at[RL], 25, 24, home(3, chain_half))
    post(is_hub, V.at[RB], V.at[RL], 24, 24, home(2, chain_half))

    @pl.when(is_last)
    def _():
        got(V.at[GL], 22)

        @pl.when(is_a3)
        def _():
            got(W.at[POUT], 20)

        value = mm(W[POUT], V[GL])
        V[TB] = mm(W[jnp.where(is_a, CT, T3)], value)

    post(is_last, V.at[TB], V.at[TL], 26, 23, home(3, chain_half))
    post(is_last & goes_on, V.at[TB], V.at[ENT], 27, 25, 32 * (6 + chain_half) + residue + 1)

    @pl.when(is_two)
    def _():
        got(V.at[PL], 21)
        V[TA] = mm(W[CT], V[PL])

    post(is_two, V.at[TA], V.at[TL], 21, 23, home(2, chain_half))
    post(is_two, V.at[TA], V.at[ENT], 22, 25, 32 * (4 + chain_half) + residue + 1)

    @pl.when(~is_first_home)
    def _():
        got(V.at[TL], 23)
        got(V.at[RL], 24)

    through_copy = pltpu.make_async_copy(V.at[TL], through_out.at[0], local.at[3])
    reflected_copy = pltpu.make_async_copy(V.at[RL], reflected_out.at[0], local.at[4])
    through_copy.start()
    reflected_copy.start()

    @pl.when(me >= 1)
    def _():
        got(V.at[ENT], 25)

    @pl.when(me == 0)
    def _():
        V[ENT] = incident_ref[...]

    depth[...] = jnp.dot(maps_left[...], right(V[ENT]), preferred_element_type=F32).reshape(
        DEPTHS, M, INC
    )
    depth_copy = pltpu.make_async_copy(depth, depth_out.at[0], local.at[5])
    depth_copy.start()

    sent(sections[2].at[0], 2)
    sent(sections[3].at[0], 3)
    for condition, source, s in finals:
        @pl.when(condition)
        def _(source=source, s=s):
            sent(source, s)

    through_copy.wait()
    reflected_copy.wait()
    depth_copy.wait()


def per_device(front_reflect, front_through, back_reflect, back_through, depth_maps, incident):
    anywhere = pl.BlockSpec(memory_space=pl.ANY)
    return pl.pallas_call(
        kernel,
        out_shape=(
            jax.ShapeDtypeStruct((1, M, INC), F32),
            jax.ShapeDtypeStruct((1, M, INC), F32),
            jax.ShapeDtypeStruct((1, DEPTHS, M, INC), F32),
        ),
        in_specs=[anywhere] * 5 + [pl.BlockSpec(memory_space=pltpu.VMEM)],
        out_specs=(anywhere,) * 3,
        scratch_shapes=[
            pltpu.VMEM((BLOCKS, M, M), F32),
            pltpu.VMEM((VECS, M, INC), F32),
            pltpu.VMEM((DEPTHS, M, M), F32),
            pltpu.VMEM((DEPTHS * M, 3 * M), BF16),
            pltpu.VMEM((DEPTHS, M, INC), F32),
            pltpu.SemaphoreType.DMA((31,)),
            pltpu.SemaphoreType.DMA((26,)),
            pltpu.SemaphoreType.DMA((6,)),
        ],
        compiler_params=pltpu.CompilerParams(
            collective_id=0, has_side_effects=True, vmem_limit_bytes=56 * 2**20
        ),
        name="chains",
    )(front_reflect, front_through, back_reflect, back_through, depth_maps, incident)


def solution(mesh):
    in_specs = (
        P("sec", None, None),
        P("sec", None, None),
        P("sec", None, None),
        P("sec", None, None),
        P("sec", None, None, None),
        P(),
    )
    out_specs = (P("sec", None, None), P("sec", None, None), P("sec", None, None, None))
    return jax.shard_map(
        per_device, mesh=mesh, in_specs=in_specs, out_specs=out_specs, check_vma=False
    )
```

time: 177 us -> 114 us (0.64)
  the two profiles are of different devices: /device:TPU:2 before, /device:TPU:29 now
where the time goes in v1:
time: 114 us
  Pallas kernels  108 us (95%)
  local copies, waits for them, and re-layouts  5.29 us (5%)
    pallas_call x1, Pallas kernels, per_device(): pl.pallas_call(kernel, out_shape=(jax.ShapeDtypeStruct((1, M, INC), F32),...  108 us
    unnamed x3, local copies, waits for them, and re-layouts  5.29 us

profile of v1, /device:TPU:29, one launch (start us, length us, event | category | flops | bytes accessed | tf_op | source)
XLA Modules:
  0.0 114.2 jit_solution(4973764003676788707)
XLA Ops:
  0.6 108.3 %chains.1 = (f32[1,384,128]{2,1,0:T(8,128)}, f32[1,384,128]{2,1,0:T(8,128)}, f32[1,4,384,128]{3,2,1,0:T(8,128)}) custom-call(f32[1,384,384]{2,1,0:T(8,128)} %reflect_ref.1, f32[1,384,384]{2,1,0:T(8,128)} %through_ref.1, f32[1,384,384]{2,1,0:T(8,128)} %mirror_ref.1, f32[1,384,384]{2,1,0:T(8,128)} %back_ref.1, f32[1,4,384,384]{3,2,1,0:T(8,128)} %maps_ref.1, ...), custom_call_target="tpu_custom_call" | custom-call | tf_op jit(solution)/shard_map/chains/pallas_call | solution.py:441
  108.9 1.6 %copy.12 = f32[1,384,128]{2,1,0:T(8,128)} copy(f32[1,384,128]{2,1,0:T(8,128)} %get-tuple-element.6) | data formatting | bytes 393216
  110.6 1.6 %copy.13 = f32[1,384,128]{2,1,0:T(8,128)} copy(f32[1,384,128]{2,1,0:T(8,128)} %get-tuple-element.7) | data formatting | bytes 393216
  112.2 2.1 %copy.14 = f32[1,4,384,128]{3,2,1,0:T(8,128)} copy(f32[1,4,384,128]{3,2,1,0:T(8,128)} %get-tuple-element.8) | data formatting | bytes 1572864

commit v2 on v1

v2 whole, which is shorter than its diff:
```python
import functools

import jax
import jax.numpy as jnp
from jax import lax
from jax.experimental import pallas as pl
from jax.experimental.pallas import tpu as pltpu
from jax.sharding import PartitionSpec as P


F32, BF16 = jnp.float32, jnp.bfloat16
MESH = pl.DeviceIdType.MESH
M, INC, DEPTHS = 384, 128, 4

FQ, FR, FT, FU, LQ, LR, LT, LU = range(8)
CQ, CR, CT, CU = range(8, 12)
DQ, DR, DT, DU, R6, T6 = range(12, 18)
HQ, HU, RIN, ROUT, POUT, R23, Q01, U01, T3, P3, TX, TM, TRP = range(18, 31)
BLOCKS = 31
HT, HR, T01, R01, G2, P1, RB, RC, TA, TB, PL, GL, TL, RL, ENT = range(15)
VECS = 15


def halves(x):
    high = x.astype(BF16)
    return high, (x - high.astype(F32)).astype(BF16)


def left(x):
    high, low = halves(x)
    return jnp.concatenate([high, low, high], axis=1)


def right(x):
    high, low = halves(x)
    return jnp.concatenate([high, high, low], axis=0)


def mm(a, b):
    return jnp.dot(left(a), right(b), preferred_element_type=F32)


def spread(mirror, reflect):
    bounce = mm(mirror, reflect)
    return bounce, bounce + mm(bounce, bounce)


def summed(bounce, both, value):
    partial_value = value + mm(both, value)
    return partial_value, value + mm(bounce, partial_value)


def forward(former, latter_reflect):
    mirror, reflect, through, back = former
    bounce, both = spread(mirror, latter_reflect)
    g_through = summed(bounce, both, through)[1]
    return reflect + mm(back, mm(latter_reflect, g_through)), g_through


def applied(mirror, back, field, reflected, latter_reflect):
    bounce = mm(mirror, latter_reflect)
    value = field
    for _ in range(3):
        value = field + mm(bounce, value)
    return value, reflected + mm(back, mm(latter_reflect, value))


def joined(mirror, back, field, reflected, latter):
    own_mirror, own_reflect, own_through, own_back = latter
    cut = field.shape[1]
    bounce, both = spread(mirror, own_reflect)
    value = jnp.concatenate([field, mm(mirror, own_back)], axis=1)
    partial_value, full_value = summed(bounce, both, value)
    through = mm(own_through, full_value)
    turned = mm(own_reflect, jnp.concatenate([full_value[:, :cut], partial_value[:, cut:]], axis=1))
    returned = mm(back, jnp.concatenate([turned[:, :cut], own_back + turned[:, cut:]], axis=1))
    return (
        through[:, :cut],
        reflected + returned[:, :cut],
        own_mirror + through[:, cut:],
        returned[:, cut:],
    )


def index_of(x, y, z, c):
    return ((y * 4 + x) * 8 + z) * 2 + c


def middle_x(x, c):
    return lax.rem(x + jnp.where(x // 2 == c, 1, 3), 4)


def producer(k_half, y, middle, z):
    at = jnp.where(y == 3, 2 + k_half, y)
    return index_of(middle, at, z, 1 - k_half)


def kernel(
    reflect_ref, through_ref, mirror_ref, back_ref, incident_ref,
    through_out, reflected_out, entering_out,
    W, V, send, recv, local,
):
    me = lax.axis_index("sec")
    c, z, x, y = me % 2, (me // 2) % 8, (me // 16) % 4, me // 64
    x_half = x // 2
    middle = middle_x(x, c)
    base = 1 - x % 2
    group_c = jnp.where(x % 2 == 1, x_half, 1 - x_half)
    residue = base * 16 + z * 2 + group_c
    chain_half = 1 - c

    def col(at_y, at_c):
        return index_of(x, at_y, z, at_c)

    def home(at_y, half):
        return index_of(base + 2 * half, at_y, z, group_c)

    is_a = c == 0
    is_mid = is_a | (y == 0) | (y == 2)
    is_hub = (is_a & (y == 1)) | ((c == 1) & (y == 0))
    is_two = y == 2
    is_a0, is_a2, is_a3 = is_a & (y == 0), is_a & (y == 2), is_a & (y == 3)
    is_b0, is_b2 = (c == 1) & (y == 0), (c == 1) & (y == 2)
    is_a1, is_b1 = is_a & (y == 1), (c == 1) & (y == 1)
    is_last = is_a3 | is_b2
    is_first_home = (x_half == 0) & (y == 0)

    barrier = pltpu.get_barrier_semaphore()

    def greet(condition, device):
        @pl.when(condition)
        def _():
            pl.semaphore_signal(barrier, inc=1, device_id=(device,), device_id_type=MESH)

    def count(condition, n=1):
        return jnp.where(condition, n, 0)

    greet(is_a, home(y, 0))
    greet(is_a, home(y, 1))
    expected = 1
    greet(is_b0 | is_b2, col(y // 2 + 1, 0))
    expected += count(is_a & ((y == 1) | (y == 2)))
    greet(is_b0 | is_b2, col(y // 2, 0))
    expected += count(is_a & (y < 2))
    greet(is_b0, home(0, 0))
    expected += count(is_first_home)
    greet(is_b2, col(3, 0))
    expected += count(is_a3)
    greet(y == 1, col(0, c))
    expected += count(is_a0)
    greet(is_a & ((y == 1) | (y == 2)), col(y + 1, 0))
    greet(is_b0, col(2, 1))
    expected += count((is_a & (y >= 2)) | is_b2)
    greet(is_two, col(1 - c, c))
    expected += count(is_hub)
    greet(is_a3, col(1, 0))
    expected += count(is_a1)
    greet(is_a3, col(2, 0))
    expected += count(is_a2)
    greet((y == 0) & (x_half == 1), index_of(middle, 0, z, 0))
    expected += count(is_a0)
    greet((y >= 2) | ((y == 1) & (x_half == 1)), index_of(middle, x_half, z, 1 - x_half))
    expected += count(is_hub, 3)
    greet((y == 1) & (x_half == 0), index_of(middle, 1, z, 1))
    expected += count(is_b1)
    greet(y >= 2, producer(x_half, y, middle, z))
    expected += count(is_two) + count(is_last)
    before = jnp.maximum(me - 1, 0)
    bc, bz, bx, by = before % 2, (before // 2) % 8, (before // 16) % 4, before // 64
    first_before = (by == 0) & (bx // 2 == 0)
    greet(
        me >= 1,
        jnp.where(first_before, before, producer(bx // 2, by, middle_x(bx, bc), bz)),
    )
    goes_on = ~(is_a3 & (residue == 31))
    expected += count(is_first_home) + count(is_a0) + count(y == 1) + count(is_two)
    expected += count(is_last & goes_on)

    @pl.when(is_first_home)
    def _():
        pltpu.make_async_copy(through_ref.at[0], W.at[T3], local.at[1]).start()
        pltpu.make_async_copy(reflect_ref.at[0], W.at[P3], local.at[2]).start()

    pl.semaphore_wait(barrier, expected)

    other = lax.rem(me + 1, lax.axis_size("sec"))

    def message(source, target, s, r, device):
        return pltpu.make_async_remote_copy(
            src_ref=source, dst_ref=target, send_sem=send.at[s], recv_sem=recv.at[r],
            device_id=(device,), device_id_type=MESH,
        )

    finals = []

    def post(condition, source, target, s, r, device):
        @pl.when(condition)
        def _():
            message(source, target, s, r, device).start()

        finals.append((condition, source, s))

    def got(target, r):
        message(target, target, 0, r, other).wait_recv()

    def sent(source, s):
        message(source, source, s, 0, other).wait_send()

    sections = (mirror_ref, reflect_ref, through_ref, back_ref)
    middle_a = index_of(middle, y, z, 0)

    def rows(block, half):
        return W.at[block, pl.ds(half * (M // 2), M // 2)]

    def piece(part, half):
        return sections[part].at[0, pl.ds(half * (M // 2), M // 2)]

    def slot(block, half):
        return 2 * block + half

    def first_send(part, half):
        message(
            piece(part, half), rows(4 * x_half + part, half), 2 * part + half,
            slot(4 * x_half + part, half), middle_a,
        ).start()

    def turned(third):
        return (3, 2) if third else (2, 3)

    def later_send(order, half):
        @pl.when(y == 0)
        def _():
            first_send(turned(order == 2)[0], half)

        @pl.when(y > 0)
        def _():
            first_send(order, half)

    def pass_on(part, half, who):
        @pl.when(who)
        def _():
            got(rows(FQ + part, half), slot(FQ + part, half))
            got(rows(LQ + part, half), slot(LQ + part, half))

        at = 8 + 2 * part + half
        post(who & ((y == 1) | (y == 2)), rows(FQ + part, half), rows(LQ + part, half), at,
             slot(LQ + part, half), col(2 * (y - 1), 1))
        post(who & (y < 2), rows(LQ + part, half), rows(FQ + part, half), at + 8,
             slot(FQ + part, half), col(2 * y, 1))
        post(who & (y == 2), rows(LQ + part, half), rows(DQ + part, half), at + 8,
             slot(8 + part, half), col(2, 1))
        if part in (0, 3):
            first = 0 if part == 0 else 1
            post(who & (y == 0), rows(FQ + part, half), rows(HQ + first, half), at,
                 slot(14 + first, half), col(0, 1))
        else:
            post(who & (y == 3), rows(FQ + part, half), rows(R6 + part - 1, half), at,
                 slot(12 + part - 1, half), col(2, 1))

    def both_halves(block, receive):
        for half in (0, 1):
            got(rows(block, half), slot(receive, half))

    for part in (0, 1):
        for half in (0, 1):
            first_send(part, half)

    @pl.when(is_first_home)
    def _():
        pltpu.make_async_copy(through_ref.at[0], W.at[T3], local.at[1]).wait()
        pltpu.make_async_copy(reflect_ref.at[0], W.at[P3], local.at[2]).wait()
        V[TL] = mm(W[T3], incident_ref[...])
        V[RL] = mm(W[P3], incident_ref[...])

    post(is_first_home, V.at[TL], V.at[HT], 40, 36, index_of(middle, 0, z, 1))
    post(is_first_home, V.at[RL], V.at[HR], 41, 37, index_of(middle, 0, z, 1))
    post(is_first_home, V.at[TL], V.at[ENT], 42, 45, other)

    for part in (0, 1):
        for half in (0, 1):
            pass_on(part, half, is_a)
            sent(piece(part, half), 2 * part + half)
            later_send(part + 2, half)

    @pl.when(is_mid)
    def _():
        @pl.when(c == 1)
        def _():
            for part in (0, 1):
                both_halves(FQ + part, FQ + part)
                both_halves(LQ + part, LQ + part)

        bounce, both = spread(W[FQ], W[LR])
        W[TX] = bounce
        W[TM] = both

    for half in (0, 1):
        pass_on(2, half, is_a & (y > 0))
        pass_on(3, half, is_a0)

    @pl.when(is_a0)
    def _():
        partial_value, full_value = summed(W[TX], W[TM], mm(W[FQ], W[LU]))
        W[TRP] = full_value
        W[CU] = mm(W[FU], W[LU] + mm(W[LR], partial_value))

    post(is_a0, W.at[CU], W.at[HU], 27, 35, col(1, 0))

    @pl.when(is_mid & ~is_a0)
    def _():
        @pl.when(c == 1)
        def _():
            both_halves(FT, FT)
            both_halves(LT, LT)

        g_through = summed(W[TX], W[TM], W[FT])[1]
        W[CT] = mm(W[LT], g_through)
        W[TRP] = mm(W[LR], g_through)

    for half in (0, 1):
        pass_on(3, half, is_a & (y > 0))
        pass_on(2, half, is_a0)

    @pl.when(is_a0)
    def _():
        W[CQ] = W[LQ] + mm(W[LT], W[TRP])

    post(is_a0, W.at[CQ], W.at[HQ], 26, 34, col(1, 0))

    @pl.when(is_a0)
    def _():
        value = summed(W[TX], W[TM], mm(W[FT], incident_ref[...]))[1]
        V[T01] = mm(W[LT], value)
        V[R01] = mm(W[FR], incident_ref[...]) + mm(W[FU], mm(W[LR], value))

    @pl.when(is_b2)
    def _():
        for part in range(4):
            both_halves(DQ + part, 8 + part)
        both_halves(R6, 12)
        both_halves(T6, 13)
        W[RIN], W[P3] = forward((W[DQ], W[DR], W[DT], W[DU]), W[R6])

    @pl.when(is_mid & ~is_a0)
    def _():
        @pl.when(c == 1)
        def _():
            both_halves(FU, FU)
            both_halves(LU, LU)

        W[CR] = W[FR] + mm(W[FU], W[TRP])

    post((is_a & (y >= 2)) | is_b2, W.at[CR], W.at[RIN], 24, 38,
         jnp.where(is_a, col(y - 1, 0), col(0, 1)))

    @pl.when(is_mid & ~is_a0)
    def _():
        partial_value, full_value = summed(W[TX], W[TM], mm(W[FQ], W[LU]))
        W[CQ] = W[LQ] + mm(W[LT], full_value)
        W[CU] = mm(W[FU], W[LU] + mm(W[LR], partial_value))

    post(is_a0, V.at[T01], V.at[HT], 28, 36, col(1, 0))
    post(is_a0, V.at[R01], V.at[HR], 29, 37, col(1, 0))
    post(is_a0, V.at[pl.ds(T01, 2)], V.at[pl.ds(TL, 2)], 30, 43, home(0, 1))
    post(is_a0, V.at[T01], V.at[ENT], 31, 45, 32 + residue + 1)

    def turn(step, carry):
        @pl.when((is_hub | is_two) & (step == 2 * c))
        def _():
            @pl.when(~is_b2)
            def _():
                got(W.at[RIN], 38)

            W[ROUT], W[POUT] = forward((W[CQ], W[CR], W[CT], W[CU]), W[RIN])

            @pl.when(is_two)
            def _():
                message(W.at[ROUT], W.at[R23], 25, 39, col(1 - c, c)).start()

            @pl.when(is_a2)
            def _():
                message(W.at[POUT], W.at[POUT], 32, 40, col(3, 0)).start()

        @pl.when(is_hub & (step == 1))
        def _():
            got(V.at[HT], 36)
            got(V.at[HR], 37)

            @pl.when(is_a)
            def _():
                got(W.at[HQ], 34)
                got(W.at[HU], 35)

            @pl.when(c == 1)
            def _():
                both_halves(HQ, 14)
                both_halves(HU, 15)

            V[T01], V[R01], W[Q01], W[U01] = joined(
                W[HQ], W[HU], V[HT], V[HR], (W[CQ], W[CR], W[CT], W[CU])
            )

            @pl.when(is_a)
            def _():
                message(V.at[pl.ds(T01, 2)], V.at[pl.ds(TL, 2)], 30, 43, home(1, 1)).start()
                message(V.at[T01], V.at[ENT], 31, 45, 32 * 3 + residue + 1).start()

            @pl.when(c == 1)
            def _():
                message(V.at[pl.ds(T01, 2)], V.at[pl.ds(T01, 2)], 30, 46, col(1, 1)).start()

        return carry

    lax.fori_loop(0, 3, turn, 0)
    finals.append((is_two, W.at[ROUT], 25))
    finals.append((is_a2, W.at[POUT], 32))
    finals.append((is_hub, V.at[pl.ds(T01, 2)], 30))
    finals.append((is_a1, V.at[T01], 31))

    @pl.when(is_b1)
    def _():
        got(V.at[pl.ds(T01, 2)], 46)

    post(is_b1, V.at[pl.ds(T01, 2)], V.at[pl.ds(TL, 2)], 30, 43, home(1, 0))
    post(is_b1, V.at[T01], V.at[ENT], 31, 45, 32 * 2 + residue + 1)

    @pl.when(is_b2)
    def _():
        W[T3] = mm(W[T6], W[P3])

    @pl.when(is_hub)
    def _():
        got(W.at[R23], 39)
        V[G2], V[RC] = applied(W[Q01], W[U01], V[T01], V[R01], W[R23])
        value, V[RB] = applied(W[HQ], W[HU], V[HT], V[HR], W[ROUT])
        V[P1] = mm(W[POUT], value)

    post(is_hub, V.at[G2], V.at[GL], 33, 42, jnp.where(is_a, col(3, 0), col(2, 1)))
    post(is_hub, V.at[P1], V.at[PL], 34, 41, col(2, c))
    post(is_hub, V.at[RC], V.at[RL], 35, 44, home(3, chain_half))
    post(is_hub, V.at[RB], V.at[RL], 36, 44, home(2, chain_half))

    @pl.when(is_last)
    def _():
        got(V.at[GL], 42)

        @pl.when(is_a3)
        def _():
            got(W.at[POUT], 40)

        value = mm(W[POUT], V[GL])
        V[TB] = mm(W[jnp.where(is_a, CT, T3)], value)

    post(is_last, V.at[TB], V.at[TL], 37, 43, home(3, chain_half))
    post(is_last & goes_on, V.at[TB], V.at[ENT], 38, 45, 32 * (6 + chain_half) + residue + 1)

    @pl.when(is_two)
    def _():
        got(V.at[PL], 41)
        V[TA] = mm(W[CT], V[PL])

    post(is_two, V.at[TA], V.at[TL], 30, 43, home(2, chain_half))
    post(is_two, V.at[TA], V.at[ENT], 31, 45, 32 * (4 + chain_half) + residue + 1)

    @pl.when((y < 2) & ~is_first_home)
    def _():
        got(V.at[pl.ds(TL, 2)], 43)

    @pl.when(y >= 2)
    def _():
        got(V.at[TL], 43)
        got(V.at[RL], 44)

    through_copy = pltpu.make_async_copy(V.at[TL], through_out, local.at[3])
    reflected_copy = pltpu.make_async_copy(V.at[RL], reflected_out, local.at[4])
    through_copy.start()
    reflected_copy.start()

    @pl.when(me >= 1)
    def _():
        got(V.at[ENT], 45)

    @pl.when(me == 0)
    def _():
        V[ENT] = incident_ref[...]

    entering_copy = pltpu.make_async_copy(V.at[ENT], entering_out, local.at[5])
    entering_copy.start()

    for part in (2, 3):
        for half in (0, 1):
            sent(piece(part, half), 2 * part + half)
    for condition, source, s in finals:
        @pl.when(condition)
        def _(source=source, s=s):
            sent(source, s)

    through_copy.wait()
    reflected_copy.wait()
    entering_copy.wait()


def fields_kernel(through_ref, reflected_ref, entering_ref, maps_ref,
                  through_out, reflected_out, depth_out):
    @pl.when(pl.program_id(0) == 0)
    def _():
        through_out[0] = through_ref[...]
        reflected_out[0] = reflected_ref[...]

    depth_out[0, 0] = mm(maps_ref[0, 0], entering_ref[...])


def per_device(front_reflect, front_through, back_reflect, back_through, depth_maps, incident):
    anywhere = pl.BlockSpec(memory_space=pl.ANY)
    field = jax.ShapeDtypeStruct((M, INC), F32)
    through, reflected, entering = pl.pallas_call(
        kernel,
        out_shape=(field,) * 3,
        in_specs=[pl.BlockSpec(memory_space=pltpu.HBM)] * 4 + [pl.BlockSpec(memory_space=pltpu.VMEM)],
        out_specs=(anywhere,) * 3,
        scratch_shapes=[
            pltpu.VMEM((BLOCKS, M, M), F32),
            pltpu.VMEM((VECS, M, INC), F32),
            pltpu.SemaphoreType.DMA((43,)),
            pltpu.SemaphoreType.DMA((47,)),
            pltpu.SemaphoreType.DMA((6,)),
        ],
        compiler_params=pltpu.CompilerParams(
            collective_id=0, has_side_effects=True, vmem_limit_bytes=44 * 2**20
        ),
        name="chains",
    )(front_reflect, front_through, back_reflect, back_through, incident)
    whole = pl.BlockSpec((M, INC), lambda j: (0, 0))
    out = pl.BlockSpec((1, M, INC), lambda j: (0, 0, 0))
    return pl.pallas_call(
        fields_kernel,
        grid=(DEPTHS,),
        out_shape=(
            jax.ShapeDtypeStruct((1, M, INC), F32),
            jax.ShapeDtypeStruct((1, M, INC), F32),
            jax.ShapeDtypeStruct((1, DEPTHS, M, INC), F32),
        ),
        in_specs=[whole, whole, whole, pl.BlockSpec((1, 1, M, M), lambda j: (0, j, 0, 0))],
        out_specs=(out, out, pl.BlockSpec((1, 1, M, INC), lambda j: (0, j, 0, 0))),
        name="depths",
    )(through, reflected, entering, depth_maps)


def solution(mesh):
    in_specs = (
        P("sec", None, None),
        P("sec", None, None),
        P("sec", None, None),
        P("sec", None, None),
        P("sec", None, None, None),
        P(),
    )
    out_specs = (P("sec", None, None), P("sec", None, None), P("sec", None, None, None))
    return jax.shard_map(
        per_device, mesh=mesh, in_specs=in_specs, out_specs=out_specs, check_vma=False
    )
```

time: 114 us -> 102 us (0.89)
  the two profiles are of different devices: /device:TPU:29 before, /device:TPU:209 now
where the time goes in v2:
time: 102 us
  Pallas kernels  94.1 us (92%)
  local copies, waits for them, and re-layouts  7.18 us (7%)
    pallas_call x1, Pallas kernels, per_device(): pl.pallas_call(kernel, out_shape=(field,) * 3, in_specs=[pl.BlockSpec(mem...  89.6 us
    unnamed x16, local copies, waits for them, and re-layouts  7.18 us
    pallas_call x1, Pallas kernels, per_device(): pl.pallas_call(fields_kernel, grid=(DEPTHS,), out_shape=(jax.ShapeDtypeSt...  4.52 us

profile of v2, /device:TPU:209, one launch (start us, length us, event | category | flops | bytes accessed | tf_op | source)
XLA Modules:
  0.0 101.9 jit_solution(3143201624160789078)
XLA Ops:
  0.6 0.0 copy-start
  0.6 1.1 %copy-done = f32[1,384,384]{2,1,0:T(8,128)S(1)} copy-done((f32[1,384,384]{2,1,0:T(8,128)S(1)}, f32[1,384,384]{2,1,0:T(8,128)}, u32[]{:S(2)}) %copy-start) | copy-done | bytes 589848
  1.7 0.0 copy-start.1
  1.7 1.1 %copy-done.1 = f32[1,384,384]{2,1,0:T(8,128)S(1)} copy-done((f32[1,384,384]{2,1,0:T(8,128)S(1)}, f32[1,384,384]{2,1,0:T(8,128)}, u32[]{:S(2)}) %copy-start.1) | copy-done | bytes 589848
  2.8 0.0 copy-start.2
  2.8 1.1 %copy-done.2 = f32[1,384,384]{2,1,0:T(8,128)S(1)} copy-done((f32[1,384,384]{2,1,0:T(8,128)S(1)}, f32[1,384,384]{2,1,0:T(8,128)}, u32[]{:S(2)}) %copy-start.2) | copy-done | bytes 589848
  3.8 0.0 copy-start.3
  3.8 1.1 %copy-done.3 = f32[1,384,384]{2,1,0:T(8,128)S(1)} copy-done((f32[1,384,384]{2,1,0:T(8,128)S(1)}, f32[1,384,384]{2,1,0:T(8,128)}, u32[]{:S(2)}) %copy-start.3) | copy-done | bytes 589848
  4.9 0.0 copy-start.4
  4.9 0.9 copy-done.4
  5.8 89.6 %chains.1 = (f32[384,128]{1,0:T(8,128)S(1)}, f32[384,128]{1,0:T(8,128)S(1)}, f32[384,128]{1,0:T(8,128)S(1)}) custom-call(f32[1,384,384]{2,1,0:T(8,128)S(1)} %copy-done, f32[1,384,384]{2,1,0:T(8,128)S(1)} %copy-done.1, f32[1,384,384]{2,1,0:T(8,128)S(1)} %copy-done.2, f32[1,384,384]{2,1,0:T(8,128)S(1)} %copy-done.3, f32[384,128]{1,0:T(8,128)S(1)} %copy-done.4), custom_call_target="tpu_custom_call" | custom-call | tf_op jit(solution)/shard_map/chains/pallas_call | solution.py:516
  95.4 0.0 copy-start.5
  95.4 0.7 copy-done.5
  96.1 0.0 copy-start.6
  96.1 0.7 copy-done.6
  96.7 0.0 copy-start.7
  96.7 0.7 copy-done.7
  97.4 4.5 %depths.1 = (f32[1,384,128]{2,1,0:T(8,128)}, f32[1,384,128]{2,1,0:T(8,128)}, f32[1,4,384,128]{3,2,1,0:T(8,128)}) custom-call(f32[384,128]{1,0:T(8,128)} %copy-done.5, f32[384,128]{1,0:T(8,128)} %copy-done.6, f32[384,128]{1,0:T(8,128)} %copy-done.7, f32[1,4,384,384]{3,2,1,0:T(8,128)} %maps_ref.1), custom_call_target="tpu_custom_call" | custom-call | tf_op jit(solution)/shard_map/depths/pallas_call | solution.py:535
Async XLA Ops:
  0.6 1.1 %copy-start = (f32[1,384,384]{2,1,0:T(8,128)S(1)}, f32[1,384,384]{2,1,0:T(8,128)}, u32[]{:S(2)}) copy-start(f32[1,384,384]{2,1,0:T(8,128)} %reflect_ref.1) | copy-start | bytes 1769476
  1.7 1.1 %copy-start.1 = (f32[1,384,384]{2,1,0:T(8,128)S(1)}, f32[1,384,384]{2,1,0:T(8,128)}, u32[]{:S(2)}) copy-start(f32[1,384,384]{2,1,0:T(8,128)} %through_ref.1) | copy-start | bytes 1769476
  2.8 1.1 %copy-start.2 = (f32[1,384,384]{2,1,0:T(8,128)S(1)}, f32[1,384,384]{2,1,0:T(8,128)}, u32[]{:S(2)}) copy-start(f32[1,384,384]{2,1,0:T(8,128)} %mirror_ref.1) | copy-start | bytes 1769476
  3.8 1.1 %copy-start.3 = (f32[1,384,384]{2,1,0:T(8,128)S(1)}, f32[1,384,384]{2,1,0:T(8,128)}, u32[]{:S(2)}) copy-start(f32[1,384,384]{2,1,0:T(8,128)} %back_ref.1) | copy-start | bytes 1769476
  4.9 0.9 copy-start.4
  95.4 0.7 copy-start.5
  96.1 0.7 copy-start.6
  96.7 0.7 copy-start.7

commit v3 on v2

--- a/solution.py
+++ b/solution.py
@@ -17,8 +17,8 @@
 DQ, DR, DT, DU, R6, T6 = range(12, 18)
 HQ, HU, RIN, ROUT, POUT, R23, Q01, U01, T3, P3, TX, TM, TRP = range(18, 31)
 BLOCKS = 31
-HT, HR, T01, R01, G2, P1, RB, RC, TA, TB, PL, GL, TL, RL, ENT = range(15)
-VECS = 15
+HT, HR, T01, R01, G2, G3, P1, RB, RC, TA, TB, PL, GL, TL, RL, ENT = range(16)
+VECS = 16
 
 
 def halves(x):
@@ -57,12 +57,11 @@
     return reflect + mm(back, mm(latter_reflect, g_through)), g_through
 
 
-def applied(mirror, back, field, reflected, latter_reflect):
-    bounce = mm(mirror, latter_reflect)
+def bounced(bounce, field):
     value = field
     for _ in range(3):
         value = field + mm(bounce, value)
-    return value, reflected + mm(back, mm(latter_reflect, value))
+    return value
 
 
 def joined(mirror, back, field, reflected, latter):
@@ -96,9 +95,9 @@
 
 
 def kernel(
-    reflect_ref, through_ref, mirror_ref, back_ref, incident_ref,
-    through_out, reflected_out, entering_out,
-    W, V, send, recv, local,
+    reflect_ref, through_ref, mirror_ref, back_ref, maps_ref, incident_ref,
+    through_out, reflected_out, depth_out,
+    W, V, maps, maps_left, depth, send, recv, local,
 ):
     me = lax.axis_index("sec")
     c, z, x, y = me % 2, (me // 2) % 8, (me // 16) % 4, me // 64
@@ -122,6 +121,7 @@
     is_a0, is_a2, is_a3 = is_a & (y == 0), is_a & (y == 2), is_a & (y == 3)
     is_b0, is_b2 = (c == 1) & (y == 0), (c == 1) & (y == 2)
     is_a1, is_b1 = is_a & (y == 1), (c == 1) & (y == 1)
+    is_b3 = (c == 1) & (y == 3)
     is_last = is_a3 | is_b2
     is_first_home = (x_half == 0) & (y == 0)
 
@@ -151,6 +151,10 @@
     greet(is_a & ((y == 1) | (y == 2)), col(y + 1, 0))
     greet(is_b0, col(2, 1))
     expected += count((is_a & (y >= 2)) | is_b2)
+    greet(is_b3, col(2, 1))
+    expected += count(is_b2)
+    greet(is_b0, col(3, 1))
+    expected += count(is_b3)
     greet(is_two, col(1 - c, c))
     expected += count(is_hub)
     greet(is_a3, col(1, 0))
@@ -181,6 +185,8 @@
         pltpu.make_async_copy(through_ref.at[0], W.at[T3], local.at[1]).start()
         pltpu.make_async_copy(reflect_ref.at[0], W.at[P3], local.at[2]).start()
 
+    maps_copy = pltpu.make_async_copy(maps_ref.at[0], maps, local.at[0])
+    maps_copy.start()
     pl.semaphore_wait(barrier, expected)
 
     other = lax.rem(me + 1, lax.axis_size("sec"))
@@ -276,6 +282,10 @@
     post(is_first_home, V.at[RL], V.at[HR], 41, 37, index_of(middle, 0, z, 1))
     post(is_first_home, V.at[TL], V.at[ENT], 42, 45, other)
 
+    maps_copy.wait()
+    for j in range(DEPTHS):
+        maps_left[j * M : (j + 1) * M, :] = left(maps[j])
+
     for part in (0, 1):
         for half in (0, 1):
             pass_on(part, half, is_a)
@@ -375,7 +385,9 @@
 
             @pl.when(is_two)
             def _():
-                message(W.at[ROUT], W.at[R23], 25, 39, col(1 - c, c)).start()
+                for half in (0, 1):
+                    message(rows(ROUT, half), rows(R23, half), 25 + 18 * half, 39 + 8 * half,
+                            col(1 + 2 * c, c)).start()
 
             @pl.when(is_a2)
             def _():
@@ -412,11 +424,19 @@
         return carry
 
     lax.fori_loop(0, 3, turn, 0)
-    finals.append((is_two, W.at[ROUT], 25))
+    finals.append((is_two, rows(ROUT, 0), 25))
+    finals.append((is_two, rows(ROUT, 1), 43))
     finals.append((is_a2, W.at[POUT], 32))
     finals.append((is_hub, V.at[pl.ds(T01, 2)], 30))
     finals.append((is_a1, V.at[T01], 31))
 
+    for half in (0, 1):
+        @pl.when(is_b3)
+        def _():
+            got(rows(R23, half), 39 + 8 * half)
+
+        post(is_b3, rows(R23, half), rows(R23, half), 25 + 18 * half, 39 + 8 * half, col(0, 1))
+
     @pl.when(is_b1)
     def _():
         got(V.at[pl.ds(T01, 2)], 46)
@@ -424,43 +444,61 @@
     post(is_b1, V.at[pl.ds(T01, 2)], V.at[pl.ds(TL, 2)], 30, 43, home(1, 0))
     post(is_b1, V.at[T01], V.at[ENT], 31, 45, 32 * 2 + residue + 1)
 
-    @pl.when(is_b2)
-    def _():
-        W[T3] = mm(W[T6], W[P3])
-
     @pl.when(is_hub)
     def _():
-        got(W.at[R23], 39)
-        V[G2], V[RC] = applied(W[Q01], W[U01], V[T01], V[R01], W[R23])
-        value, V[RB] = applied(W[HQ], W[HU], V[HT], V[HR], W[ROUT])
-        V[P1] = mm(W[POUT], value)
-
-    post(is_hub, V.at[G2], V.at[GL], 33, 42, jnp.where(is_a, col(3, 0), col(2, 1)))
+        bounce = mm(W[HQ], W[ROUT])
+        V[G2] = bounced(bounce, V[HT])
+        V[P1] = mm(W[POUT], V[G2])
+
     post(is_hub, V.at[P1], V.at[PL], 34, 41, col(2, c))
+
+    @pl.when(is_hub)
+    def _():
+        V[RB] = V[HR] + mm(W[HU], mm(W[ROUT], V[G2]))
+
+    post(is_hub, V.at[RB], V.at[RL], 36, 44, home(2, chain_half))
+
+    @pl.when(is_last)
+    def _():
+        @pl.when(is_a3)
+        def _():
+            got(W.at[POUT], 40)
+            W[T3] = mm(W[CT], W[POUT])
+
+        @pl.when(is_b2)
+        def _():
+            W[T3] = mm(W[T6], mm(W[P3], W[POUT]))
+
+    @pl.when(is_hub)
+    def _():
+        got(rows(R23, 0), 39)
+        got(rows(R23, 1), 47)
+        bounce = mm(W[Q01], W[R23])
+        V[G3] = bounced(bounce, V[T01])
+
+    post(is_hub, V.at[G3], V.at[GL], 33, 42, jnp.where(is_a, col(3, 0), col(2, 1)))
+
+    @pl.when(is_hub)
+    def _():
+        V[RC] = V[R01] + mm(W[U01], mm(W[R23], V[G3]))
+
     post(is_hub, V.at[RC], V.at[RL], 35, 44, home(3, chain_half))
-    post(is_hub, V.at[RB], V.at[RL], 36, 44, home(2, chain_half))
-
-    @pl.when(is_last)
-    def _():
-        got(V.at[GL], 42)
-
-        @pl.when(is_a3)
-        def _():
-            got(W.at[POUT], 40)
-
-        value = mm(W[POUT], V[GL])
-        V[TB] = mm(W[jnp.where(is_a, CT, T3)], value)
-
-    post(is_last, V.at[TB], V.at[TL], 37, 43, home(3, chain_half))
-    post(is_last & goes_on, V.at[TB], V.at[ENT], 38, 45, 32 * (6 + chain_half) + residue + 1)
 
     @pl.when(is_two)
     def _():
         got(V.at[PL], 41)
         V[TA] = mm(W[CT], V[PL])
 
+    post(is_two, V.at[TA], V.at[ENT], 31, 45, 32 * (4 + chain_half) + residue + 1)
     post(is_two, V.at[TA], V.at[TL], 30, 43, home(2, chain_half))
-    post(is_two, V.at[TA], V.at[ENT], 31, 45, 32 * (4 + chain_half) + residue + 1)
+
+    @pl.when(is_last)
+    def _():
+        got(V.at[GL], 42)
+        V[TB] = mm(W[T3], V[GL])
+
+    post(is_last & goes_on, V.at[TB], V.at[ENT], 38, 45, 32 * (6 + chain_half) + residue + 1)
+    post(is_last, V.at[TB], V.at[TL], 37, 43, home(3, chain_half))
 
     @pl.when((y < 2) & ~is_first_home)
     def _():
@@ -471,8 +509,8 @@
         got(V.at[TL], 43)
         got(V.at[RL], 44)
 
-    through_copy = pltpu.make_async_copy(V.at[TL], through_out, local.at[3])
-    reflected_copy = pltpu.make_async_copy(V.at[RL], reflected_out, local.at[4])
+    through_copy = pltpu.make_async_copy(V.at[TL], through_out.at[0], local.at[3])
+    reflected_copy = pltpu.make_async_copy(V.at[RL], reflected_out.at[0], local.at[4])
     through_copy.start()
     reflected_copy.start()
 
@@ -484,8 +522,11 @@
     def _():
         V[ENT] = incident_ref[...]
 
-    entering_copy = pltpu.make_async_copy(V.at[ENT], entering_out, local.at[5])
-    entering_copy.start()
+    depth[...] = jnp.dot(maps_left[...], right(V[ENT]), preferred_element_type=F32).reshape(
+        DEPTHS, M, INC
+    )
+    depth_copy = pltpu.make_async_copy(depth, depth_out.at[0], local.at[5])
+    depth_copy.start()
 
     for part in (2, 3):
         for half in (0, 1):
@@ -497,53 +538,58 @@
 
     through_copy.wait()
     reflected_copy.wait()
-    entering_copy.wait()
-
-
-def fields_kernel(through_ref, reflected_ref, entering_ref, maps_ref,
-                  through_out, reflected_out, depth_out):
-    @pl.when(pl.program_id(0) == 0)
-    def _():
-        through_out[0] = through_ref[...]
-        reflected_out[0] = reflected_ref[...]
-
-    depth_out[0, 0] = mm(maps_ref[0, 0], entering_ref[...])
+    depth_copy.wait()
+
+
+def results_kernel(through_ref, reflected_ref, depth_ref, through_out, reflected_out, depth_out, local):
+    copies = [
+        pltpu.make_async_copy(through_ref, through_out, local.at[0]),
+        pltpu.make_async_copy(reflected_ref, reflected_out, local.at[1]),
+    ]
+    for j in range(DEPTHS):
+        copies.append(pltpu.make_async_copy(depth_ref.at[0, j], depth_out.at[0, j], local.at[2 + j]))
+    for copy in copies:
+        copy.start()
+    for copy in copies:
+        copy.wait()
 
 
 def per_device(front_reflect, front_through, back_reflect, back_through, depth_maps, incident):
     anywhere = pl.BlockSpec(memory_space=pl.ANY)
-    field = jax.ShapeDtypeStruct((M, INC), F32)
-    through, reflected, entering = pl.pallas_call(
+    results = (
+        jax.ShapeDtypeStruct((1, M, INC), F32),
+        jax.ShapeDtypeStruct((1, M, INC), F32),
+        jax.ShapeDtypeStruct((1, DEPTHS, M, INC), F32),
+    )
+    made = pl.pallas_call(
         kernel,
-        out_shape=(field,) * 3,
-        in_specs=[pl.BlockSpec(memory_space=pltpu.HBM)] * 4 + [pl.BlockSpec(memory_space=pltpu.VMEM)],
+        out_shape=results,
+        in_specs=[anywhere] * 5 + [pl.BlockSpec(memory_space=pltpu.VMEM)],
         out_specs=(anywhere,) * 3,
         scratch_shapes=[
             pltpu.VMEM((BLOCKS, M, M), F32),
             pltpu.VMEM((VECS, M, INC), F32),
-            pltpu.SemaphoreType.DMA((43,)),
-            pltpu.SemaphoreType.DMA((47,)),
+            pltpu.VMEM((DEPTHS, M, M), F32),
+            pltpu.VMEM((DEPTHS * M, 3 * M), BF16),
+            pltpu.VMEM((DEPTHS, M, INC), F32),
+            pltpu.SemaphoreType.DMA((44,)),
+            pltpu.SemaphoreType.DMA((48,)),
             pltpu.SemaphoreType.DMA((6,)),
         ],
         compiler_params=pltpu.CompilerParams(
-            collective_id=0, has_side_effects=True, vmem_limit_bytes=44 * 2**20
+            collective_id=0, has_side_effects=True, vmem_limit_bytes=60 * 2**20
         ),
         name="chains",
-    )(front_reflect, front_through, back_reflect, back_through, incident)
-    whole = pl.BlockSpec((M, INC), lambda j: (0, 0))
-    out = pl.BlockSpec((1, M, INC), lambda j: (0, 0, 0))
+    )(front_reflect, front_through, back_reflect, back_through, depth_maps, incident)
     return pl.pallas_call(
-        fields_kernel,
-        grid=(DEPTHS,),
-        out_shape=(
-            jax.ShapeDtypeStruct((1, M, INC), F32),
-            jax.ShapeDtypeStruct((1, M, INC), F32),
-            jax.ShapeDtypeStruct((1, DEPTHS, M, INC), F32),
-        ),
-        in_specs=[whole, whole, whole, pl.BlockSpec((1, 1, M, M), lambda j: (0, j, 0, 0))],
-        out_specs=(out, out, pl.BlockSpec((1, 1, M, INC), lambda j: (0, j, 0, 0))),
-        name="depths",
-    )(through, reflected, entering, depth_maps)
+        results_kernel,
+        out_shape=results,
+        in_specs=[anywhere] * 3,
+        out_specs=(anywhere,) * 3,
+        scratch_shapes=[pltpu.SemaphoreType.DMA((2 + DEPTHS,))],
+        compiler_params=pltpu.CompilerParams(vmem_limit_bytes=60 * 2**20),
+        name="results",
+    )(*made)
 
 
 def solution(mesh):

time: 102 us -> 125 us (1.23)
  the two profiles are of different devices: /device:TPU:209 before, /device:TPU:120 now
where the time goes in v3:
time: 125 us; the launch traced here: 124 us
  Pallas kernels  123 us (98%)
    pallas_call x1, Pallas kernels, per_device(): pl.pallas_call(kernel, out_shape=results, in_specs=[anywhere] * 5 + [pl.B...  86.4 us
    pallas_call x1, Pallas kernels, per_device(): pl.pallas_call(results_kernel, out_shape=results, in_specs=[anywhere] * 3...  36.9 us

profile of v3, /device:TPU:120, one launch (start us, length us, event | category | flops | bytes accessed | tf_op | source)
XLA Modules:
  0.0 124.1 jit_solution(6965173570364338477)
XLA Ops:
  0.6 86.4 %chains.1 = (f32[1,384,128]{2,1,0:T(8,128)}, f32[1,384,128]{2,1,0:T(8,128)}, f32[1,4,384,128]{3,2,1,0:T(8,128)}) custom-call(f32[1,384,384]{2,1,0:T(8,128)} %reflect_ref.1, f32[1,384,384]{2,1,0:T(8,128)} %through_ref.1, f32[1,384,384]{2,1,0:T(8,128)} %mirror_ref.1, f32[1,384,384]{2,1,0:T(8,128)} %back_ref.1, f32[1,4,384,384]{3,2,1,0:T(8,128)} %maps_ref.1, ...), custom_call_target="tpu_custom_call" | custom-call | tf_op jit(solution)/shard_map/chains/pallas_call | solution.py:564
  87.0 36.9 %results.1 = (f32[1,384,128]{2,1,0:T(8,128)}, f32[1,384,128]{2,1,0:T(8,128)}, f32[1,4,384,128]{3,2,1,0:T(8,128)}) custom-call(f32[1,384,128]{2,1,0:T(8,128)} %get-tuple-element.6.through_ref, f32[1,384,128]{2,1,0:T(8,128)} %get-tuple-element.7.reflected_ref, f32[1,4,384,128]{3,2,1,0:T(8,128)} %get-tuple-element.8.depth_ref), custom_call_target="tpu_custom_call" | custom-call | tf_op jit(solution)/shard_map/results/pallas_call | solution.py:584

commit v4 on v3

--- a/solution.py
+++ b/solution.py
@@ -327,8 +327,33 @@
         W[CT] = mm(W[LT], g_through)
         W[TRP] = mm(W[LR], g_through)
 
+    @pl.when(is_b2)
+    def _():
+        for part in (0, 1, 2):
+            both_halves(DQ + part, 8 + part)
+        both_halves(R6, 12)
+        bounce, both = spread(W[DQ], W[R6])
+        W[P3] = summed(bounce, both, W[DT])[1]
+        W[T3] = mm(W[R6], W[P3])
+
     for half in (0, 1):
         pass_on(3, half, is_a & (y > 0))
+
+        @pl.when(is_mid & ~is_a0)
+        def _(half=half):
+            here = pl.ds(half * (M // 2), M // 2)
+
+            @pl.when(c == 1)
+            def _():
+                got(rows(FU, half), slot(FU, half))
+                got(rows(LU, half), slot(LU, half))
+
+            W[CR, here] = W[FR, here] + mm(W[FU, here], W[TRP])
+
+        post((is_a & (y >= 2)) | is_b2, rows(CR, half), rows(RIN, half), 24 + 20 * half, 38 + 10 * half,
+             jnp.where(is_a, col(y - 1, 0), col(0, 1)))
+
+    for half in (0, 1):
         pass_on(2, half, is_a0)
 
     @pl.when(is_a0)
@@ -345,23 +370,8 @@
 
     @pl.when(is_b2)
     def _():
-        for part in range(4):
-            both_halves(DQ + part, 8 + part)
-        both_halves(R6, 12)
-        both_halves(T6, 13)
-        W[RIN], W[P3] = forward((W[DQ], W[DR], W[DT], W[DU]), W[R6])
-
-    @pl.when(is_mid & ~is_a0)
-    def _():
-        @pl.when(c == 1)
-        def _():
-            both_halves(FU, FU)
-            both_halves(LU, LU)
-
-        W[CR] = W[FR] + mm(W[FU], W[TRP])
-
-    post((is_a & (y >= 2)) | is_b2, W.at[CR], W.at[RIN], 24, 38,
-         jnp.where(is_a, col(y - 1, 0), col(0, 1)))
+        both_halves(DU, 11)
+        W[RIN] = W[DR] + mm(W[DU], W[T3])
 
     @pl.when(is_mid & ~is_a0)
     def _():
@@ -379,7 +389,8 @@
         def _():
             @pl.when(~is_b2)
             def _():
-                got(W.at[RIN], 38)
+                got(rows(RIN, 0), 38)
+                got(rows(RIN, 1), 48)
 
             W[ROUT], W[POUT] = forward((W[CQ], W[CR], W[CT], W[CU]), W[RIN])
 
@@ -467,6 +478,7 @@
 
         @pl.when(is_b2)
         def _():
+            both_halves(T6, 13)
             W[T3] = mm(W[T6], mm(W[P3], W[POUT]))
 
     @pl.when(is_hub)
@@ -541,17 +553,10 @@
     depth_copy.wait()
 
 
-def results_kernel(through_ref, reflected_ref, depth_ref, through_out, reflected_out, depth_out, local):
-    copies = [
-        pltpu.make_async_copy(through_ref, through_out, local.at[0]),
-        pltpu.make_async_copy(reflected_ref, reflected_out, local.at[1]),
-    ]
-    for j in range(DEPTHS):
-        copies.append(pltpu.make_async_copy(depth_ref.at[0, j], depth_out.at[0, j], local.at[2 + j]))
-    for copy in copies:
-        copy.start()
-    for copy in copies:
-        copy.wait()
+def results_kernel(through_ref, reflected_ref, depth_ref, through_out, reflected_out, depth_out):
+    through_out[...] = through_ref[...]
+    reflected_out[...] = reflected_ref[...]
+    depth_out[...] = depth_ref[...]
 
 
 def per_device(front_reflect, front_through, back_reflect, back_through, depth_maps, incident):
@@ -572,8 +577,8 @@
             pltpu.VMEM((DEPTHS, M, M), F32),
             pltpu.VMEM((DEPTHS * M, 3 * M), BF16),
             pltpu.VMEM((DEPTHS, M, INC), F32),
-            pltpu.SemaphoreType.DMA((44,)),
-            pltpu.SemaphoreType.DMA((48,)),
+            pltpu.SemaphoreType.DMA((45,)),
+            pltpu.SemaphoreType.DMA((49,)),
             pltpu.SemaphoreType.DMA((6,)),
         ],
         compiler_params=pltpu.CompilerParams(
@@ -584,10 +589,8 @@
     return pl.pallas_call(
         results_kernel,
         out_shape=results,
-        in_specs=[anywhere] * 3,
-        out_specs=(anywhere,) * 3,
-        scratch_shapes=[pltpu.SemaphoreType.DMA((2 + DEPTHS,))],
-        compiler_params=pltpu.CompilerParams(vmem_limit_bytes=60 * 2**20),
+        in_specs=[pl.BlockSpec(memory_space=pltpu.VMEM)] * 3,
+        out_specs=(pl.BlockSpec(memory_space=pltpu.VMEM),) * 3,
         name="results",
     )(*made)
 

time: 125 us -> 88.4 us (0.71)
  Pallas kernels: 123 us -> 87.6 us
    pallas_call x1, Pallas kernels: 36.9 us -> 2.36 us  [per_device(): pl.pallas_call(results_kernel, out_shape=results, in_specs=[pl.BlockSpec(...]
where the time goes in v4:
time: 88.4 us; the launch traced here: 88.2 us
  Pallas kernels  87.6 us (99%)
    pallas_call x1, Pallas kernels, per_device(): pl.pallas_call(kernel, out_shape=results, in_specs=[anywhere] * 5 + [pl.B...  85.2 us
    pallas_call x1, Pallas kernels, per_device(): pl.pallas_call(results_kernel, out_shape=results, in_specs=[pl.BlockSpec(...  2.36 us

profile of v4, /device:TPU:120, one launch (start us, length us, event | category | flops | bytes accessed | tf_op | source)
XLA Modules:
  0.0 88.2 jit_solution(6709244408801951325)
XLA Ops:
  0.6 85.2 %chains.1 = (f32[1,384,128]{2,1,0:T(8,128)}, f32[1,384,128]{2,1,0:T(8,128)}, f32[1,4,384,128]{3,2,1,0:T(8,128)}) custom-call(f32[1,384,384]{2,1,0:T(8,128)} %reflect_ref.1, f32[1,384,384]{2,1,0:T(8,128)} %through_ref.1, f32[1,384,384]{2,1,0:T(8,128)} %mirror_ref.1, f32[1,384,384]{2,1,0:T(8,128)} %back_ref.1, f32[1,4,384,384]{3,2,1,0:T(8,128)} %maps_ref.1, ...), custom_call_target="tpu_custom_call" | custom-call | tf_op jit(solution)/shard_map/chains/pallas_call | solution.py:569
  85.9 2.4 %results.1 = (f32[1,384,128]{2,1,0:T(8,128)}, f32[1,384,128]{2,1,0:T(8,128)}, f32[1,4,384,128]{3,2,1,0:T(8,128)}) custom-call(f32[1,384,128]{2,1,0:T(8,128)} %get-tuple-element.6.through_ref, f32[1,384,128]{2,1,0:T(8,128)} %get-tuple-element.7.reflected_ref, f32[1,4,384,128]{3,2,1,0:T(8,128)} %get-tuple-element.8.depth_ref), custom_call_target="tpu_custom_call" | custom-call | tf_op jit(solution)/shard_map/results/pallas_call | solution.py:589

commit v5 on v4

--- a/solution.py
+++ b/solution.py
@@ -50,35 +50,11 @@
     return partial_value, value + mm(bounce, partial_value)
 
 
-def forward(former, latter_reflect):
-    mirror, reflect, through, back = former
-    bounce, both = spread(mirror, latter_reflect)
-    g_through = summed(bounce, both, through)[1]
-    return reflect + mm(back, mm(latter_reflect, g_through)), g_through
-
-
 def bounced(bounce, field):
     value = field
     for _ in range(3):
         value = field + mm(bounce, value)
     return value
-
-
-def joined(mirror, back, field, reflected, latter):
-    own_mirror, own_reflect, own_through, own_back = latter
-    cut = field.shape[1]
-    bounce, both = spread(mirror, own_reflect)
-    value = jnp.concatenate([field, mm(mirror, own_back)], axis=1)
-    partial_value, full_value = summed(bounce, both, value)
-    through = mm(own_through, full_value)
-    turned = mm(own_reflect, jnp.concatenate([full_value[:, :cut], partial_value[:, cut:]], axis=1))
-    returned = mm(back, jnp.concatenate([turned[:, :cut], own_back + turned[:, cut:]], axis=1))
-    return (
-        through[:, :cut],
-        reflected + returned[:, :cut],
-        own_mirror + through[:, cut:],
-        returned[:, cut:],
-    )
 
 
 def index_of(x, y, z, c):
@@ -121,7 +97,6 @@
     is_a0, is_a2, is_a3 = is_a & (y == 0), is_a & (y == 2), is_a & (y == 3)
     is_b0, is_b2 = (c == 1) & (y == 0), (c == 1) & (y == 2)
     is_a1, is_b1 = is_a & (y == 1), (c == 1) & (y == 1)
-    is_b3 = (c == 1) & (y == 3)
     is_last = is_a3 | is_b2
     is_first_home = (x_half == 0) & (y == 0)
 
@@ -151,10 +126,6 @@
     greet(is_a & ((y == 1) | (y == 2)), col(y + 1, 0))
     greet(is_b0, col(2, 1))
     expected += count((is_a & (y >= 2)) | is_b2)
-    greet(is_b3, col(2, 1))
-    expected += count(is_b2)
-    greet(is_b0, col(3, 1))
-    expected += count(is_b3)
     greet(is_two, col(1 - c, c))
     expected += count(is_hub)
     greet(is_a3, col(1, 0))
@@ -335,6 +306,8 @@
         bounce, both = spread(W[DQ], W[R6])
         W[P3] = summed(bounce, both, W[DT])[1]
         W[T3] = mm(W[R6], W[P3])
+        both_halves(DU, 11)
+        W[RIN] = W[DR] + mm(W[DU], W[T3])
 
     for half in (0, 1):
         pass_on(3, half, is_a & (y > 0))
@@ -367,11 +340,6 @@
         value = summed(W[TX], W[TM], mm(W[FT], incident_ref[...]))[1]
         V[T01] = mm(W[LT], value)
         V[R01] = mm(W[FR], incident_ref[...]) + mm(W[FU], mm(W[LR], value))
-
-    @pl.when(is_b2)
-    def _():
-        both_halves(DU, 11)
-        W[RIN] = W[DR] + mm(W[DU], W[T3])
 
     @pl.when(is_mid & ~is_a0)
     def _():
@@ -392,13 +360,17 @@
                 got(rows(RIN, 0), 38)
                 got(rows(RIN, 1), 48)
 
-            W[ROUT], W[POUT] = forward((W[CQ], W[CR], W[CT], W[CU]), W[RIN])
-
-            @pl.when(is_two)
-            def _():
-                for half in (0, 1):
+            bounce, both = spread(W[CQ], W[RIN])
+            W[POUT] = summed(bounce, both, W[CT])[1]
+            W[TRP] = mm(W[RIN], W[POUT])
+            for half in (0, 1):
+                here = pl.ds(half * (M // 2), M // 2)
+                W[ROUT, here] = W[CR, here] + mm(W[CU, here], W[TRP])
+
+                @pl.when(is_two)
+                def _(half=half):
                     message(rows(ROUT, half), rows(R23, half), 25 + 18 * half, 39 + 8 * half,
-                            col(1 + 2 * c, c)).start()
+                            col(1 - c, c)).start()
 
             @pl.when(is_a2)
             def _():
@@ -406,22 +378,40 @@
 
         @pl.when(is_hub & (step == 1))
         def _():
+            @pl.when(is_a)
+            def _():
+                got(W.at[HQ], 34)
+
+            @pl.when(c == 1)
+            def _():
+                both_halves(HQ, 14)
+
+            bounce, both = spread(W[HQ], W[CR])
+            W[TX] = bounce
+            W[TM] = both
+            W[TRP] = mm(W[HQ], W[CU])
             got(V.at[HT], 36)
+            value = jnp.concatenate([V[HT], W[TRP]], axis=1)
+            partial_value, full_value = summed(W[TX], W[TM], value)
+            through = mm(W[CT], full_value)
+            V[T01] = through[:, :INC]
+            W[Q01] = W[CQ] + through[:, INC:]
+            back = mm(W[CR], jnp.concatenate([full_value[:, :INC], partial_value[:, INC:]], axis=1))
+            V[G2] = back[:, :INC]
+            W[TRP] = W[CU] + back[:, INC:]
+
+            @pl.when(is_a)
+            def _():
+                got(W.at[HU], 35)
+
+            @pl.when(c == 1)
+            def _():
+                both_halves(HU, 15)
+
+            returned = mm(W[HU], jnp.concatenate([V[G2], W[TRP]], axis=1))
+            W[U01] = returned[:, INC:]
             got(V.at[HR], 37)
-
-            @pl.when(is_a)
-            def _():
-                got(W.at[HQ], 34)
-                got(W.at[HU], 35)
-
-            @pl.when(c == 1)
-            def _():
-                both_halves(HQ, 14)
-                both_halves(HU, 15)
-
-            V[T01], V[R01], W[Q01], W[U01] = joined(
-                W[HQ], W[HU], V[HT], V[HR], (W[CQ], W[CR], W[CT], W[CU])
-            )
+            V[R01] = V[HR] + returned[:, :INC]
 
             @pl.when(is_a)
             def _():
@@ -441,13 +431,6 @@
     finals.append((is_hub, V.at[pl.ds(T01, 2)], 30))
     finals.append((is_a1, V.at[T01], 31))
 
-    for half in (0, 1):
-        @pl.when(is_b3)
-        def _():
-            got(rows(R23, half), 39 + 8 * half)
-
-        post(is_b3, rows(R23, half), rows(R23, half), 25 + 18 * half, 39 + 8 * half, col(0, 1))
-
     @pl.when(is_b1)
     def _():
         got(V.at[pl.ds(T01, 2)], 46)
@@ -455,19 +438,33 @@
     post(is_b1, V.at[pl.ds(T01, 2)], V.at[pl.ds(TL, 2)], 30, 43, home(1, 0))
     post(is_b1, V.at[T01], V.at[ENT], 31, 45, 32 * 2 + residue + 1)
 
-    @pl.when(is_hub)
-    def _():
-        bounce = mm(W[HQ], W[ROUT])
-        V[G2] = bounced(bounce, V[HT])
-        V[P1] = mm(W[POUT], V[G2])
-
-    post(is_hub, V.at[P1], V.at[PL], 34, 41, col(2, c))
-
-    @pl.when(is_hub)
-    def _():
-        V[RB] = V[HR] + mm(W[HU], mm(W[ROUT], V[G2]))
-
-    post(is_hub, V.at[RB], V.at[RL], 36, 44, home(2, chain_half))
+    def last_fields(step, carry):
+        @pl.when(is_hub & (step == chain_half))
+        def _():
+            bounce = mm(W[HQ], W[ROUT])
+            V[G2] = bounced(bounce, V[HT])
+            V[P1] = mm(W[POUT], V[G2])
+            message(V.at[P1], V.at[PL], 34, 41, col(2, c)).start()
+            V[RB] = V[HR] + mm(W[HU], mm(W[ROUT], V[G2]))
+            message(V.at[RB], V.at[RL], 36, 44, home(2, chain_half)).start()
+
+        @pl.when(is_hub & (step == c))
+        def _():
+            got(rows(R23, 0), 39)
+            got(rows(R23, 1), 47)
+            bounce = mm(W[Q01], W[R23])
+            V[G3] = bounced(bounce, V[T01])
+            message(V.at[G3], V.at[GL], 33, 42, jnp.where(is_a, col(3, 0), col(2, 1))).start()
+            V[RC] = V[R01] + mm(W[U01], mm(W[R23], V[G3]))
+            message(V.at[RC], V.at[RL], 35, 44, home(3, chain_half)).start()
+
+        return carry
+
+    lax.fori_loop(0, 2, last_fields, 0)
+    finals.append((is_hub, V.at[P1], 34))
+    finals.append((is_hub, V.at[RB], 36))
+    finals.append((is_hub, V.at[G3], 33))
+    finals.append((is_hub, V.at[RC], 35))
 
     @pl.when(is_last)
     def _():
@@ -480,21 +477,6 @@
         def _():
             both_halves(T6, 13)
             W[T3] = mm(W[T6], mm(W[P3], W[POUT]))
-
-    @pl.when(is_hub)
-    def _():
-        got(rows(R23, 0), 39)
-        got(rows(R23, 1), 47)
-        bounce = mm(W[Q01], W[R23])
-        V[G3] = bounced(bounce, V[T01])
-
-    post(is_hub, V.at[G3], V.at[GL], 33, 42, jnp.where(is_a, col(3, 0), col(2, 1)))
-
-    @pl.when(is_hub)
-    def _():
-        V[RC] = V[R01] + mm(W[U01], mm(W[R23], V[G3]))
-
-    post(is_hub, V.at[RC], V.at[RL], 35, 44, home(3, chain_half))
 
     @pl.when(is_two)
     def _():

time: 88.4 us -> 86.2 us (0.975)
  Pallas kernels: 87.6 us -> 85.2 us
    pallas_call x1, Pallas kernels: 85.2 us -> 82.8 us  [per_device(): pl.pallas_call(kernel, out_shape=results, in_specs=[anywhere] * 5 + [pl.B...]
where the time goes in v5:
time: 86.2 us; the launch traced here: 85.8 us
  Pallas kernels  85.2 us (99%)
    pallas_call x1, Pallas kernels, per_device(): pl.pallas_call(kernel, out_shape=results, in_specs=[anywhere] * 5 + [pl.B...  82.8 us
    pallas_call x1, Pallas kernels, per_device(): pl.pallas_call(results_kernel, out_shape=results, in_specs=[pl.BlockSpec(...  2.36 us

profile of v5, /device:TPU:120, one launch (start us, length us, event | category | flops | bytes accessed | tf_op | source)
XLA Modules:
  0.0 85.8 jit_solution(12323778880541114764)
XLA Ops:
  0.6 82.8 %chains.1 = (f32[1,384,128]{2,1,0:T(8,128)}, f32[1,384,128]{2,1,0:T(8,128)}, f32[1,4,384,128]{3,2,1,0:T(8,128)}) custom-call(f32[1,384,384]{2,1,0:T(8,128)} %reflect_ref.1, f32[1,384,384]{2,1,0:T(8,128)} %through_ref.1, f32[1,384,384]{2,1,0:T(8,128)} %mirror_ref.1, f32[1,384,384]{2,1,0:T(8,128)} %back_ref.1, f32[1,4,384,384]{3,2,1,0:T(8,128)} %maps_ref.1, ...), custom_call_target="tpu_custom_call" | custom-call | tf_op jit(solution)/shard_map/chains/pallas_call | solution.py:551
  83.5 2.4 %results.1 = (f32[1,384,128]{2,1,0:T(8,128)}, f32[1,384,128]{2,1,0:T(8,128)}, f32[1,4,384,128]{3,2,1,0:T(8,128)}) custom-call(f32[1,384,128]{2,1,0:T(8,128)} %get-tuple-element.6.through_ref, f32[1,384,128]{2,1,0:T(8,128)} %get-tuple-element.7.reflected_ref, f32[1,4,384,128]{3,2,1,0:T(8,128)} %get-tuple-element.8.depth_ref), custom_call_target="tpu_custom_call" | custom-call | tf_op jit(solution)/shard_map/results/pallas_call | solution.py:571

commit v6 on v5

--- a/solution.py
+++ b/solution.py
@@ -66,8 +66,7 @@
 
 
 def producer(k_half, y, middle, z):
-    at = jnp.where(y == 3, 2 + k_half, y)
-    return index_of(middle, at, z, 1 - k_half)
+    return index_of(middle, y, z, 1 - k_half)
 
 
 def kernel(
@@ -97,7 +96,7 @@
     is_a0, is_a2, is_a3 = is_a & (y == 0), is_a & (y == 2), is_a & (y == 3)
     is_b0, is_b2 = (c == 1) & (y == 0), (c == 1) & (y == 2)
     is_a1, is_b1 = is_a & (y == 1), (c == 1) & (y == 1)
-    is_last = is_a3 | is_b2
+    is_last = y == 3
     is_first_home = (x_half == 0) & (y == 0)
 
     barrier = pltpu.get_barrier_semaphore()
@@ -128,10 +127,10 @@
     expected += count((is_a & (y >= 2)) | is_b2)
     greet(is_two, col(1 - c, c))
     expected += count(is_hub)
-    greet(is_a3, col(1, 0))
-    expected += count(is_a1)
-    greet(is_a3, col(2, 0))
-    expected += count(is_a2)
+    greet(is_last, col(1 - c, c))
+    expected += count(is_hub)
+    greet(is_last, col(2, c))
+    expected += count(is_two)
     greet((y == 0) & (x_half == 1), index_of(middle, 0, z, 0))
     expected += count(is_a0)
     greet((y >= 2) | ((y == 1) & (x_half == 1)), index_of(middle, x_half, z, 1 - x_half))
@@ -438,45 +437,71 @@
     post(is_b1, V.at[pl.ds(T01, 2)], V.at[pl.ds(TL, 2)], 30, 43, home(1, 0))
     post(is_b1, V.at[T01], V.at[ENT], 31, 45, 32 * 2 + residue + 1)
 
-    def last_fields(step, carry):
-        @pl.when(is_hub & (step == chain_half))
-        def _():
-            bounce = mm(W[HQ], W[ROUT])
-            V[G2] = bounced(bounce, V[HT])
-            V[P1] = mm(W[POUT], V[G2])
-            message(V.at[P1], V.at[PL], 34, 41, col(2, c)).start()
-            V[RB] = V[HR] + mm(W[HU], mm(W[ROUT], V[G2]))
-            message(V.at[RB], V.at[RL], 36, 44, home(2, chain_half)).start()
-
-        @pl.when(is_hub & (step == c))
-        def _():
-            got(rows(R23, 0), 39)
-            got(rows(R23, 1), 47)
-            bounce = mm(W[Q01], W[R23])
-            V[G3] = bounced(bounce, V[T01])
-            message(V.at[G3], V.at[GL], 33, 42, jnp.where(is_a, col(3, 0), col(2, 1))).start()
-            V[RC] = V[R01] + mm(W[U01], mm(W[R23], V[G3]))
-            message(V.at[RC], V.at[RL], 35, 44, home(3, chain_half)).start()
-
-        return carry
-
-    lax.fori_loop(0, 2, last_fields, 0)
+    @pl.when(is_b2)
+    def _():
+        both_halves(T6, 13)
+        W[T3] = mm(W[T6], mm(W[P3], W[POUT]))
+
+    post(is_b2, W.at[T3], W.at[T3], 32, 40, col(3, 1))
+
+    def stack_field():
+        message(V.at[G3], V.at[GL], 33, 42, col(3, c)).start()
+
+    def step_field():
+        message(V.at[P1], V.at[PL], 34, 41, col(2, c)).start()
+
+    def early_reflected():
+        V[RB] = V[HR] + mm(W[HU], mm(W[ROUT], V[G2]))
+        message(V.at[RB], V.at[RL], 36, 44, home(2, chain_half)).start()
+
+    def late_reflected():
+        V[RC] = V[R01] + mm(W[U01], mm(W[R23], V[G3]))
+        message(V.at[RC], V.at[RL], 35, 44, home(3, chain_half)).start()
+
+    def arrived():
+        got(rows(R23, 0), 39)
+        got(rows(R23, 1), 47)
+
+    @pl.when(is_a1)
+    def _():
+        arrived()
+        late, early = mm(W[Q01], W[R23]), mm(W[HQ], W[ROUT])
+        late_value, early_value = V[T01], V[HT]
+        for _ in range(3):
+            late_value = V[T01] + mm(late, late_value)
+            early_value = V[HT] + mm(early, early_value)
+        V[G3] = late_value
+        V[G2] = early_value
+        stack_field()
+        V[P1] = mm(W[POUT], early_value)
+        step_field()
+        late_reflected()
+        early_reflected()
+
+    @pl.when(is_b0)
+    def _():
+        V[G2] = bounced(mm(W[HQ], W[ROUT]), V[HT])
+        V[P1] = mm(W[POUT], V[G2])
+        step_field()
+        early_reflected()
+        arrived()
+        V[G3] = bounced(mm(W[Q01], W[R23]), V[T01])
+        stack_field()
+        late_reflected()
+
     finals.append((is_hub, V.at[P1], 34))
     finals.append((is_hub, V.at[RB], 36))
     finals.append((is_hub, V.at[G3], 33))
     finals.append((is_hub, V.at[RC], 35))
 
-    @pl.when(is_last)
-    def _():
-        @pl.when(is_a3)
-        def _():
-            got(W.at[POUT], 40)
-            W[T3] = mm(W[CT], W[POUT])
-
-        @pl.when(is_b2)
-        def _():
-            both_halves(T6, 13)
-            W[T3] = mm(W[T6], mm(W[P3], W[POUT]))
+    @pl.when(is_a3)
+    def _():
+        got(W.at[POUT], 40)
+        W[T3] = mm(W[CT], W[POUT])
+
+    @pl.when(is_last & (c == 1))
+    def _():
+        got(W.at[T3], 40)
 
     @pl.when(is_two)
     def _():
@@ -535,10 +560,23 @@
     depth_copy.wait()
 
 
-def results_kernel(through_ref, reflected_ref, depth_ref, through_out, reflected_out, depth_out):
-    through_out[...] = through_ref[...]
-    reflected_out[...] = reflected_ref[...]
-    depth_out[...] = depth_ref[...]
+def results_kernel(through_ref, reflected_ref, depth_ref, through_out, reflected_out, depth_out,
+                   held, inward, outward):
+    pieces = [(through_ref.at[0], through_out.at[0]), (reflected_ref.at[0], reflected_out.at[0])]
+    pieces += [(depth_ref.at[0, j], depth_out.at[0, j]) for j in range(DEPTHS)]
+    arriving = [
+        pltpu.make_async_copy(source, held.at[i], inward.at[i]) for i, (source, _) in enumerate(pieces)
+    ]
+    leaving = [
+        pltpu.make_async_copy(held.at[i], target, outward.at[i]) for i, (_, target) in enumerate(pieces)
+    ]
+    for copy in arriving:
+        copy.start()
+    for copy, after in zip(arriving, leaving):
+        copy.wait()
+        after.start()
+    for copy in leaving:
+        copy.wait()
 
 
 def per_device(front_reflect, front_through, back_reflect, back_through, depth_maps, incident):
@@ -571,8 +609,14 @@
     return pl.pallas_call(
         results_kernel,
         out_shape=results,
-        in_specs=[pl.BlockSpec(memory_space=pltpu.VMEM)] * 3,
-        out_specs=(pl.BlockSpec(memory_space=pltpu.VMEM),) * 3,
+        in_specs=[anywhere] * 3,
+        out_specs=(anywhere,) * 3,
+        scratch_shapes=[
+            pltpu.VMEM((2 + DEPTHS, M, INC), F32),
+            pltpu.SemaphoreType.DMA((2 + DEPTHS,)),
+            pltpu.SemaphoreType.DMA((2 + DEPTHS,)),
+        ],
+        compiler_params=pltpu.CompilerParams(vmem_limit_bytes=60 * 2**20),
         name="results",
     )(*made)
 

time: 86.2 us -> 84.6 us (0.981)
  Pallas kernels: 85.2 us -> 83.7 us
    pallas_call x1, Pallas kernels: 82.8 us -> 81.5 us  [per_device(): pl.pallas_call(kernel, out_shape=results, in_specs=[anywhere] * 5 + [pl.B...]
where the time goes in v6:
time: 84.6 us; the launch traced here: 84.5 us
  Pallas kernels  83.7 us (99%)
    pallas_call x1, Pallas kernels, per_device(): pl.pallas_call(kernel, out_shape=results, in_specs=[anywhere] * 5 + [pl.B...  81.5 us
    pallas_call x1, Pallas kernels, per_device(): pl.pallas_call(results_kernel, out_shape=results, in_specs=[anywhere] * 3...  2.13 us

profile of v6, /device:TPU:120, one launch (start us, length us, event | category | flops | bytes accessed | tf_op | source)
XLA Modules:
  0.0 84.5 jit_solution(4912713684887575824)
XLA Ops:
  0.6 81.5 %chains.1 = (f32[1,384,128]{2,1,0:T(8,128)}, f32[1,384,128]{2,1,0:T(8,128)}, f32[1,4,384,128]{3,2,1,0:T(8,128)}) custom-call(f32[1,384,384]{2,1,0:T(8,128)} %reflect_ref.1, f32[1,384,384]{2,1,0:T(8,128)} %through_ref.1, f32[1,384,384]{2,1,0:T(8,128)} %mirror_ref.1, f32[1,384,384]{2,1,0:T(8,128)} %back_ref.1, f32[1,4,384,384]{3,2,1,0:T(8,128)} %maps_ref.1, ...), custom_call_target="tpu_custom_call" | custom-call | tf_op jit(solution)/shard_map/chains/pallas_call | solution.py:589
  82.2 2.1 %results.1 = (f32[1,384,128]{2,1,0:T(8,128)}, f32[1,384,128]{2,1,0:T(8,128)}, f32[1,4,384,128]{3,2,1,0:T(8,128)}) custom-call(f32[1,384,128]{2,1,0:T(8,128)} %get-tuple-element.6.through_ref, f32[1,384,128]{2,1,0:T(8,128)} %get-tuple-element.7.reflected_ref, f32[1,4,384,128]{3,2,1,0:T(8,128)} %get-tuple-element.8.depth_ref), custom_call_target="tpu_custom_call" | custom-call | tf_op jit(solution)/shard_map/results/pallas_call | solution.py:609

commit v7 on v6

--- a/solution.py
+++ b/solution.py
@@ -286,17 +286,6 @@
 
     post(is_a0, W.at[CU], W.at[HU], 27, 35, col(1, 0))
 
-    @pl.when(is_mid & ~is_a0)
-    def _():
-        @pl.when(c == 1)
-        def _():
-            both_halves(FT, FT)
-            both_halves(LT, LT)
-
-        g_through = summed(W[TX], W[TM], W[FT])[1]
-        W[CT] = mm(W[LT], g_through)
-        W[TRP] = mm(W[LR], g_through)
-
     @pl.when(is_b2)
     def _():
         for part in (0, 1, 2):
@@ -305,6 +294,20 @@
         bounce, both = spread(W[DQ], W[R6])
         W[P3] = summed(bounce, both, W[DT])[1]
         W[T3] = mm(W[R6], W[P3])
+
+    @pl.when(is_mid & ~is_a0)
+    def _():
+        @pl.when(c == 1)
+        def _():
+            both_halves(FT, FT)
+            both_halves(LT, LT)
+
+        g_through = summed(W[TX], W[TM], W[FT])[1]
+        W[CT] = mm(W[LT], g_through)
+        W[TRP] = mm(W[LR], g_through)
+
+    @pl.when(is_b2)
+    def _():
         both_halves(DU, 11)
         W[RIN] = W[DR] + mm(W[DU], W[T3])
 

time: 84.6 us -> 83.7 us (0.989)
  Pallas kernels: 83.7 us -> 82.8 us
    pallas_call x1, Pallas kernels: 81.5 us -> 80.6 us  [per_device(): pl.pallas_call(kernel, out_shape=results, in_specs=[anywhere] * 5 + [pl.B...]
where the time goes in v7:
time: 83.7 us; the launch traced here: 83.6 us
  Pallas kernels  82.8 us (99%)
    pallas_call x1, Pallas kernels, per_device(): pl.pallas_call(kernel, out_shape=results, in_specs=[anywhere] * 5 + [pl.B...  80.6 us
    pallas_call x1, Pallas kernels, per_device(): pl.pallas_call(results_kernel, out_shape=results, in_specs=[anywhere] * 3...  2.13 us

profile of v7, /device:TPU:120, one launch (start us, length us, event | category | flops | bytes accessed | tf_op | source)
XLA Modules:
  0.0 83.6 jit_solution(4075318205459808718)
XLA Ops:
  0.6 80.6 %chains.1 = (f32[1,384,128]{2,1,0:T(8,128)}, f32[1,384,128]{2,1,0:T(8,128)}, f32[1,4,384,128]{3,2,1,0:T(8,128)}) custom-call(f32[1,384,384]{2,1,0:T(8,128)} %reflect_ref.1, f32[1,384,384]{2,1,0:T(8,128)} %through_ref.1, f32[1,384,384]{2,1,0:T(8,128)} %mirror_ref.1, f32[1,384,384]{2,1,0:T(8,128)} %back_ref.1, f32[1,4,384,384]{3,2,1,0:T(8,128)} %maps_ref.1, ...), custom_call_target="tpu_custom_call" | custom-call | tf_op jit(solution)/shard_map/chains/pallas_call | solution.py:592
  81.3 2.1 %results.1 = (f32[1,384,128]{2,1,0:T(8,128)}, f32[1,384,128]{2,1,0:T(8,128)}, f32[1,4,384,128]{3,2,1,0:T(8,128)}) custom-call(f32[1,384,128]{2,1,0:T(8,128)} %get-tuple-element.6.through_ref, f32[1,384,128]{2,1,0:T(8,128)} %get-tuple-element.7.reflected_ref, f32[1,4,384,128]{3,2,1,0:T(8,128)} %get-tuple-element.8.depth_ref), custom_call_target="tpu_custom_call" | custom-call | tf_op jit(solution)/shard_map/results/pallas_call | solution.py:612

commit v8 on v7

--- a/solution.py
+++ b/solution.py
@@ -486,11 +486,11 @@
         V[G2] = bounced(mm(W[HQ], W[ROUT]), V[HT])
         V[P1] = mm(W[POUT], V[G2])
         step_field()
-        early_reflected()
         arrived()
         V[G3] = bounced(mm(W[Q01], W[R23]), V[T01])
         stack_field()
         late_reflected()
+        early_reflected()
 
     finals.append((is_hub, V.at[P1], 34))
     finals.append((is_hub, V.at[RB], 36))

time: 83.7 us -> 83.7 us (level)
  no operation moved by 1% of the time
where the time goes in v8:
time: 83.7 us; the launch traced here: 83.6 us
  Pallas kernels  82.8 us (99%)
    pallas_call x1, Pallas kernels, per_device(): pl.pallas_call(kernel, out_shape=results, in_specs=[anywhere] * 5 + [pl.B...  80.6 us
    pallas_call x1, Pallas kernels, per_device(): pl.pallas_call(results_kernel, out_shape=results, in_specs=[anywhere] * 3...  2.13 us

profile of v8, /device:TPU:120, one launch (start us, length us, event | category | flops | bytes accessed | tf_op | source)
XLA Modules:
  0.0 83.6 jit_solution(4265695565631386611)
XLA Ops:
  0.6 80.6 %chains.1 = (f32[1,384,128]{2,1,0:T(8,128)}, f32[1,384,128]{2,1,0:T(8,128)}, f32[1,4,384,128]{3,2,1,0:T(8,128)}) custom-call(f32[1,384,384]{2,1,0:T(8,128)} %reflect_ref.1, f32[1,384,384]{2,1,0:T(8,128)} %through_ref.1, f32[1,384,384]{2,1,0:T(8,128)} %mirror_ref.1, f32[1,384,384]{2,1,0:T(8,128)} %back_ref.1, f32[1,4,384,384]{3,2,1,0:T(8,128)} %maps_ref.1, ...), custom_call_target="tpu_custom_call" | custom-call | tf_op jit(solution)/shard_map/chains/pallas_call | solution.py:592
  81.3 2.1 %results.1 = (f32[1,384,128]{2,1,0:T(8,128)}, f32[1,384,128]{2,1,0:T(8,128)}, f32[1,4,384,128]{3,2,1,0:T(8,128)}) custom-call(f32[1,384,128]{2,1,0:T(8,128)} %get-tuple-element.6.through_ref, f32[1,384,128]{2,1,0:T(8,128)} %get-tuple-element.7.reflected_ref, f32[1,4,384,128]{3,2,1,0:T(8,128)} %get-tuple-element.8.depth_ref), custom_call_target="tpu_custom_call" | custom-call | tf_op jit(solution)/shard_map/results/pallas_call | solution.py:612
